TPU v7x, 512 devices: a whole 4x8x8 slice. The times are simulated.
512 devices in a mesh: grp: 16 (over y, z_lo), gz: 32 (over x, z_hi, core).
Axes of the slice: x: 4, y: 8, z: 8 (z_hi: 4, z_lo: 2; z = z_hi * 2 + z_lo), core: 2. Of those that a mesh axis runs over, the one named last changes fastest.
Arguments:
- features: bfloat16 [64, 4096, 256], P('gz', 'grp'), may hold values from -6 to 6
- grad_output: bfloat16 [64, 4096, 256], P('gz', 'grp'), may hold values from -24 to 24
- qkv_weight: bfloat16 [256, 768], replicated, may hold values from -5 to 5
- out_weight: bfloat16 [256, 256], replicated, may hold values from -0.375 to 0.375
- up_weight: bfloat16 [256, 512], replicated, may hold values from -0.375 to 0.375
- down_weight: bfloat16 [512, 256], replicated, may hold values from -0.25 to 0.25
- norm_gains: float32 [2, 256], replicated, may hold values from 0.5 to 8
Outputs:
- input_grad: bfloat16 [64, 4096, 256], P('gz', 'grp')
- grad_qkv: float32 [256, 768], replicated
- grad_out: float32 [256, 256], replicated
- grad_up: float32 [256, 512], replicated
- grad_down: float32 [512, 256], replicated
- grad_gains: float32 [2, 256], replicated
All inputs are finite; a program needn't handle non-finite values.
Results may differ from a plain program's by a relative error of at most 0.013.
The roundings to bfloat16 on the way count: a program that leaves them out, or rounds other values in their place, can miss the bound.
Values may be sent and summed in bfloat16 or wider, within the bound.
No kernel may reach another device: no remote copies, remote signals or barrier semaphores. Data moves between devices by JAX's collectives and lax.ppermute only.
A program may use at most 64 MiB of HBM per device.

v0:
```python
import jax
import jax.numpy as jnp
from jax import lax
from jax.sharding import PartitionSpec as P

HEADS = 8


EPS = 1e-06


def mix(form, left, right):
    return jnp.einsum(form, left, right, preferred_element_type=jnp.float32)


def normed(values, gain):
    scale = lax.rsqrt(jnp.mean(values * values, -1, keepdims=True) + EPS)
    return (values * scale * gain, scale)


def norm_back(values, scale, gain, grad):
    scaled = grad * gain
    dvalues = scale * scaled - values * scale**3 * jnp.mean(scaled * values, -1, keepdims=True)
    return (dvalues, jnp.sum(grad * values * scale, axis=0))


def attend(block, qkv_weight, out_weight, gain):
    zlen, plen, width = block.shape
    size = width // HEADS
    flat = block.astype(jnp.float32).reshape(-1, width)
    normal, scale = normed(flat, gain)
    normal_low = normal.astype(jnp.bfloat16)
    proj = (
        mix("nc,cd->nd", normal_low, qkv_weight)
        .astype(jnp.bfloat16)
        .reshape(zlen, plen, 3, HEADS, size)
    )
    query, keys, values = (proj[:, :, 0], proj[:, :, 1], proj[:, :, 2])
    scores = mix("zphd,yphd->phzy", query, keys) * size ** (-0.5)
    probs = jax.nn.softmax(scores, axis=-1)
    probs_low = probs.astype(jnp.bfloat16)
    mixed = mix("phzy,yphd->zphd", probs_low, values).astype(jnp.bfloat16).reshape(-1, width)
    result = mix("nc,cd->nd", mixed, out_weight).astype(jnp.bfloat16).reshape(zlen, plen, width)
    return (result, (flat, scale, normal_low, query, keys, values, probs, probs_low, mixed))


def attend_back(grad, saved, qkv_weight, out_weight, gain):
    flat, scale, normal_low, query, keys, values, probs, probs_low, mixed = saved
    zlen, plen, width = grad.shape
    size = width // HEADS
    grad_flat = grad.reshape(-1, width)
    g_out = mix("nc,nd->cd", mixed, grad_flat)
    dmixed = (
        mix("nd,cd->nc", grad_flat, out_weight)
        .astype(jnp.bfloat16)
        .reshape(zlen, plen, HEADS, size)
    )
    dprobs = mix("zphd,yphd->phzy", dmixed, values)
    dvalues = mix("phzy,zphd->yphd", probs_low, dmixed).astype(jnp.bfloat16)
    dscores = (
        probs * (dprobs - jnp.sum(probs * dprobs, -1, keepdims=True)) * size ** (-0.5)
    ).astype(jnp.bfloat16)
    dquery = mix("phzy,yphd->zphd", dscores, keys).astype(jnp.bfloat16)
    dkeys = mix("phzy,zphd->yphd", dscores, query).astype(jnp.bfloat16)
    dproj = jnp.stack([dquery, dkeys, dvalues], 2).reshape(-1, 3 * width)
    g_qkv = mix("nc,nd->cd", normal_low, dproj)
    dnormal = mix("nd,cd->nc", dproj, qkv_weight)
    dflat, g_gain = norm_back(flat, scale, gain, dnormal)
    return (dflat.astype(jnp.bfloat16).reshape(zlen, plen, width), g_qkv, g_out, g_gain)


def mlp_back(hidden, grad, up_weight, down_weight, gain):
    normal, scale = normed(hidden, gain)
    normal_low = normal.astype(jnp.bfloat16)
    pre = mix("nc,cf->nf", normal_low, up_weight)
    active = jax.nn.sigmoid(pre)
    gated = (pre * active).astype(jnp.bfloat16)
    g_down = mix("nf,nc->fc", gated, grad)
    dgated = mix("nc,fc->nf", grad, down_weight)
    dpre = (dgated * active * (1.0 + pre * (1.0 - active))).astype(jnp.bfloat16)
    g_up = mix("nc,nf->cf", normal_low, dpre)
    dnormal = mix("nf,cf->nc", dpre, up_weight)
    dhidden, g_gain = norm_back(hidden, scale, gain, dnormal)
    return ((grad.astype(jnp.float32) + dhidden).astype(jnp.bfloat16), g_up, g_down, g_gain)


def body(features, grad_output, qkv_weight, out_weight, up_weight, down_weight, norm_gains):
    sections, pixels, width = features.shape
    columns = lax.all_to_all(features, "gz", split_axis=1, concat_axis=0, tiled=True)
    attn, saved = attend(columns, qkv_weight, out_weight, norm_gains[0])
    attn_slab = lax.all_to_all(attn, "gz", split_axis=0, concat_axis=1, tiled=True)
    hidden = features.astype(jnp.float32).reshape(-1, width) + attn_slab.astype(
        jnp.float32
    ).reshape(-1, width)
    dhidden, g_up, g_down, g_two = mlp_back(
        hidden, grad_output.reshape(-1, width), up_weight, down_weight, norm_gains[1]
    )
    dcolumns = lax.all_to_all(
        dhidden.reshape(sections, pixels, width), "gz", split_axis=1, concat_axis=0, tiled=True
    )
    dattn, g_qkv, g_out, g_one = attend_back(dcolumns, saved, qkv_weight, out_weight, norm_gains[0])
    dattn_slab = lax.all_to_all(dattn, "gz", split_axis=0, concat_axis=1, tiled=True)
    input_grad = (
        dhidden.astype(jnp.float32).reshape(sections, pixels, width)
        + dattn_slab.astype(jnp.float32)
    ).astype(jnp.bfloat16)
    g_gains = jnp.stack([g_one, g_two])
    g_qkv, g_out, g_up, g_down, g_gains = lax.psum(
        (g_qkv, g_out, g_up, g_down, g_gains), ("grp", "gz")
    )
    factor = float(sections * lax.axis_size("gz") * pixels * lax.axis_size("grp")) ** (-0.5)
    return (
        input_grad,
        g_qkv * factor,
        g_out * factor,
        g_up * factor,
        g_down * factor,
        g_gains * factor,
    )


def solution(mesh):
    in_specs = (P("gz", "grp", None), P("gz", "grp", None), P(), P(), P(), P(), P())
    out_specs = (P("gz", "grp", None), P(), P(), P(), P(), P())
    return jax.shard_map(body, mesh=mesh, in_specs=in_specs, out_specs=out_specs, check_vma=False)
```

profile of v0, /device:TPU:1, one launch (start us, length us, event | category | flops | bytes accessed | tf_op | source)
XLA Modules:
  0.0 418.1 jit_solution(4703469996500724086)
XLA Ops:
  7.2 2.0 copy.54
  9.2 14.4 %all-to-all-start = ((bf16[2,256,256]{2,0,1:T(2,128)(2,1)}), bf16[2,256,256]{2,0,1:T(2,128)(2,1)S(1)}, u32[]{:S(2)}, u32[]{:S(2)}) async-start(bf16[2,256,256]{2,0,1:T(2,128)(2,1)} %copy.54), calls=%async_computation | async-start | bytes 524288 | tf_op jit(solution)/shard_map/all_to_all | solution.py:89
  24.3 12.7 %all-to-all-done = bf16[2,256,256]{2,0,1:T(2,128)(2,1)S(1)} async-done(((bf16[2,256,256]{2,0,1:T(2,128)(2,1)}), bf16[2,256,256]{2,0,1:T(2,128)(2,1)S(1)}, u32[]{:S(2)}, u32[]{:S(2)}) %all-to-all-start) | async-done | bytes 262176 | tf_op jit(solution)/shard_map/all_to_all | solution.py:89
  40.3 3.6 reshape.143
  43.9 2.1 fusion.75
  46.1 2.3 copy.77
  48.4 2.5 copy.76
  52.1 2.3 fusion.77
  54.3 2.0 fusion.20
  60.6 4.0 all-to-all-start.1
  65.5 12.6 %all-to-all-done.1 = bf16[64,8,256]{2,1,0:T(8,128)(2,1)S(1)} async-done(((bf16[64,8,256]{2,1,0:T(8,128)(2,1)}), bf16[64,8,256]{2,1,0:T(8,128)(2,1)S(1)}, u32[]{:S(2)}, u32[]{:S(2)}) %all-to-all-start.1) | async-done | bytes 262176 | tf_op jit(solution)/shard_map/all_to_all | solution.py:91
  82.1 3.9 all-to-all-start.2
  87.2 2.5 fusion.56
  89.7 9.9 %all-to-all-done.2 = bf16[2,256,256]{2,0,1:T(2,128)(2,1)S(1)} async-done(((bf16[2,256,256]{2,0,1:T(2,128)(2,1)}), bf16[2,256,256]{2,0,1:T(2,128)(2,1)S(1)}, u32[]{:S(2)}, u32[]{:S(2)}) %all-to-all-start.2) | async-done | bytes 262176 | tf_op jit(solution)/shard_map/all_to_all | solution.py:98
  102.5 3.1 fusion.21
  106.1 3.9 fusion.25
  110.0 3.9 fusion.22
  113.9 2.7 pad_maximum_fusion
  116.6 5.9 %copy.70 = bf16[64,8,3,8,32]{4,3,2,1,0:T(8,128)(2,1)S(1)} copy(bf16[64,8,3,8,32]{0,4,3,1,2:T(8,128)(2,1)} %pad_maximum_fusion) | data formatting | bytes 1572864 | tf_op jit(solution)/shard_map/stack | solution.py:65
  122.6 2.8 reshape.151
  129.6 4.0 all-to-all-start.3
  133.5 101.5 %psum.39 = f32[2,256]{1,0:T(2,128)S(1)} all-reduce(f32[2,256]{1,0:T(2,128)S(1)} %pad_maximum_fusion.1), channel_id=1, replica_groups=mesh['grp'=16,'gz'=32] {'grp','gz'}, use_global_device_ids=true, to_apply=%region_13.0 | all-reduce | flops 512 | bytes 4096 | tf_op jit(solution)/shard_map/psum | solution.py:108
  236.4 169.4 %all-reduce.3.cloned.1.call-done = (f32[256,768]{1,0:T(8,128)}, f32[256,256]{1,0:T(8,128)}, f32[256,512]{1,0:T(8,128)}, f32[512,256]{1,0:T(8,128)}) async-done(((f32[256,768]{1,0:T(8,128)}, f32[256,256]{1,0:T(8,128)}, f32[256,512]{1,0:T(8,128)}, f32[512,256]{1,0:T(8,128)}), (f32[256,768]{1,0:T(8,128)}, f32[256,256]{1,0:T(8,128)}, f32[256,512]{1,0:T(8,128)}, ...) | async-done | bytes 2097168 | tf_op jit(solution)/shard_map/psum | solution.py:108
  405.8 2.2 broadcast_multiply_fusion
  (101 shorter events, 27.4 us)
Async XLA Ops:
  7.2 31.9 %copy-start = (bf16[256,768]{1,0:T(8,128)(2,1)S(1)}, bf16[256,768]{1,0:T(8,128)(2,1)}, u32[]{:S(2)}) copy-start(bf16[256,768]{1,0:T(8,128)(2,1)} %param.9) | copy-start | bytes 1179652
  9.2 27.9 %all-to-all-start = ((bf16[2,256,256]{2,0,1:T(2,128)(2,1)}), bf16[2,256,256]{2,0,1:T(2,128)(2,1)S(1)}, u32[]{:S(2)}, u32[]{:S(2)}) async-start(bf16[2,256,256]{2,0,1:T(2,128)(2,1)} %copy.54), calls=%async_computation | async-start | bytes 524288 | tf_op jit(solution)/shard_map/all_to_all | solution.py:89
  46.1 4.8 %copy-start.7 = (bf16[64,8,1,8,32]{4,3,2,1,0:T(8,128)(2,1)S(1)}, bf16[64,8,1,8,32]{4,3,2,1,0:T(8,128)(2,1)}, u32[]{:S(2)}) copy-start(bf16[64,8,1,8,32]{4,3,2,1,0:T(8,128)(2,1)} %get-tuple-element.16) | copy-start | bytes 786436
  48.4 5.9 %copy-start.13 = (bf16[64,8,1,8,32]{0,4,3,1,2:T(8,128)(2,1)}, bf16[64,8,1,8,32]{0,4,3,1,2:T(8,128)(2,1)S(1)}, u32[]{:S(2)}) copy-start(bf16[64,8,1,8,32]{0,4,3,1,2:T(8,128)(2,1)S(1)} %copy.77) | copy-start | bytes 786436
  52.1 2.3 copy-start.15
  54.3 2.0 copy-start.25
  56.4 8.3 %copy-start.6 = (f32[2,32,8,256]{3,0,2,1:T(2,128)S(1)}, f32[2,32,8,256]{3,0,2,1:T(2,128)}, u32[]{:S(2)}) copy-start(f32[2,32,8,256]{3,0,2,1:T(2,128)} %copy-done.5) | copy-start | bytes 1572868
  58.0 6.7 %copy-start.21 = (f32[32,2,8]{2,1,0:T(2,128)S(1)}, f32[32,2,8]{2,1,0:T(2,128)}, u32[]{:S(2)}) copy-start(f32[32,2,8]{2,1,0:T(2,128)} %copy-done.20) | copy-start | bytes 6148
  58.7 19.6 %copy-start.4 = (bf16[2,256,256]{2,1,0:T(8,128)(2,1)S(1)}, bf16[2,256,256]{2,1,0:T(8,128)(2,1)}, u32[]{:S(2)}) copy-start(bf16[2,256,256]{2,1,0:T(8,128)(2,1)} %param.7) | copy-start | bytes 786436
  60.6 17.5 %all-to-all-start.1 = ((bf16[64,8,256]{2,1,0:T(8,128)(2,1)}), bf16[64,8,256]{2,1,0:T(8,128)(2,1)S(1)}, u32[]{:S(2)}, u32[]{:S(2)}) async-start(bf16[64,8,256]{2,1,0:T(8,128)(2,1)} %fusion.28), calls=%async_computation.1 | async-start | bytes 524288 | tf_op jit(solution)/shard_map/all_to_all | solution.py:91
  64.7 13.9 %copy-start.12 = (bf16[256,512]{1,0:T(8,128)(2,1)S(1)}, bf16[256,512]{1,0:T(8,128)(2,1)}, u32[]{:S(2)}) copy-start(bf16[256,512]{1,0:T(8,128)(2,1)} %param.11) | copy-start | bytes 786436
  81.1 8.6 %copy-start.8 = (bf16[512,256]{1,0:T(8,128)(2,1)}, bf16[512,256]{1,0:T(8,128)(2,1)S(1)}, u32[]{:S(2)}) copy-start(bf16[512,256]{1,0:T(8,128)(2,1)S(1)} %add_convert_fusion) | copy-start | bytes 786436
  82.1 17.6 %all-to-all-start.2 = ((bf16[2,256,256]{2,0,1:T(2,128)(2,1)}), bf16[2,256,256]{2,0,1:T(2,128)(2,1)S(1)}, u32[]{:S(2)}, u32[]{:S(2)}) async-start(bf16[2,256,256]{2,0,1:T(2,128)(2,1)} %copy.62), calls=%async_computation.2 | async-start | bytes 524288 | tf_op jit(solution)/shard_map/all_to_all | solution.py:98
  86.0 319.8 %all-reduce.3.cloned.1.call-start = ((), (), s32[]{:S(2)}) async-start(), calls=%async_computation.4 | async-start | bytes 4194304 | tf_op jit(solution)/shard_map/psum | solution.py:108
  87.2 13.5 %copy-start.16 = (bf16[256,256]{1,0:T(8,128)(2,1)S(1)}, bf16[256,256]{1,0:T(8,128)(2,1)}, u32[]{:S(2)}) copy-start(bf16[256,256]{1,0:T(8,128)(2,1)} %param.10) | copy-start | bytes 393220
  99.7 2.9 copy-start.26
  106.1 3.9 copy-start.14
  110.0 3.9 copy-start.19
  125.4 1.9 copy-start.10
  128.5 5.0 %copy-start.23 = (f32[256]{0:T(256)S(1)}, f32[256]{0:T(256)}, u32[]{:S(2)}) copy-start(f32[256]{0:T(256)} %get-tuple-element.6) | copy-start | bytes 3076
  128.5 107.1 %copy-start.9 = (bf16[512,256]{1,0:T(8,128)(2,1)S(1)}, bf16[512,256]{1,0:T(8,128)(2,1)}, u32[]{:S(2)}) copy-start(bf16[512,256]{1,0:T(8,128)(2,1)} %copy-done.8) | copy-start | bytes 786436
  129.6 106.0 %all-to-all-start.3 = ((bf16[64,8,256]{2,1,0:T(8,128)(2,1)}), bf16[64,8,256]{2,1,0:T(8,128)(2,1)S(1)}, u32[]{:S(2)}, u32[]{:S(2)}) async-start(bf16[64,8,256]{2,1,0:T(8,128)(2,1)} %bitcast.27), calls=%async_computation.3 | async-start | bytes 524288 | tf_op jit(solution)/shard_map/all_to_all | solution.py:102
  405.8 3.8 copy-start.18
  405.8 4.7 %copy-start.17 = (f32[512,256]{1,0:T(8,128)S(1)}, f32[512,256]{1,0:T(8,128)}, u32[]{:S(2)}) copy-start(f32[512,256]{1,0:T(8,128)} %get-tuple-element.13) | copy-start | bytes 1572868
  (8 other events, 9.2 us)
Sparse Core Ops, SparseCore 0:
  128.7 277.0 all-reduce.2
where the time goes:
time: 419 us; the launch traced here: 418 us
  waiting for transfers between devices  205 us (49%)
  blocking collectives  101 us (24%)
  local copies, waits for them, and re-layouts  30 us (7%)
  matrix products  28.4 us (7%)
  starting transfers between devices  26.4 us (6%)
  between operations  14.5 us (3%)
  other arithmetic  12.6 us (3%)
    psum x1, waiting for transfers between devices, body(): lax.psum((g_qkv, g_out, g_up, g_down, g_gains), ('grp', 'gz'))  169 us
    psum x1, blocking collectives, body(): lax.psum((g_qkv, g_out, g_up, g_down, g_gains), ('grp', 'gz'))  101 us
    dot_general x16, matrix products, mix(): return jnp.einsum(form, left, right, preferred_element_type=jnp.float32)  26.2 us
    all_to_all x1, starting transfers between devices, body(): lax.all_to_all(features, 'gz', split_axis=1, concat_axis=0, tiled=True)  14.4 us
    all_to_all x1, waiting for transfers between devices, body(): lax.all_to_all(features, 'gz', split_axis=1, concat_axis=0, tiled=True)  12.7 us
    all_to_all x1, waiting for transfers between devices, body(): lax.all_to_all(attn, 'gz', split_axis=0, concat_axis=1, tiled=True)  12.6 us
    all_to_all x1, waiting for transfers between devices, body(): lax.all_to_all(dhidden.reshape(sections, pixels, width), 'gz', split_axis...  9.9 us
    unnamed x59, local copies, waits for them, and re-layouts  9.67 us
  transfers between devices with their start and end apart: 5, of which 4 were waited for; matrix products, arithmetic and copies ran while one was open for 2% of the time, Pallas kernels for 0%

commit v1 on v0

v1 whole, which is shorter than its diff:
```python
import functools

import jax
import jax.numpy as jnp
from jax import lax
from jax.experimental import pallas as pl
from jax.experimental.pallas import tpu as pltpu
from jax.sharding import Mesh
from jax.sharding import PartitionSpec as P

HEADS = 8
EPS = 1e-06
BF, F32 = jnp.bfloat16, jnp.float32
LANES = 128
VMEM_LIMIT = 56 * 1024 * 1024


def dot(left, right, over=(1, 0)):
    return lax.dot_general(
        left, right, (((over[0],), (over[1],)), ((), ())), preferred_element_type=F32
    )


def block_kernel(
    pixels, core_ref, xg_ref, wqkv_ref, wout_ref, wup_ref, wdown_ref, gains_ref,
    dx_ref, send_ref, keep_ref, proj_ref, probs_ref, mixed_ref, dmixed_ref, dproj_ref,
):
    sources, both, width = xg_ref.shape
    half = both // 2
    rows = sources * half
    zlen = rows // pixels
    size = width // HEADS
    wide = HEADS * zlen
    hidden_units = wup_ref.shape[1]

    at = lax.broadcasted_iota(jnp.int32, (rows, rows), 0)
    to = lax.broadcasted_iota(jnp.int32, (rows, rows), 1)
    order = jnp.where(to == (at % zlen) * pixels + at // zlen, 1.0, 0.0).astype(BF)
    x = dot(order, xg_ref[:, :half, :].reshape(rows, width))
    g = dot(order, xg_ref[:, half:, :].reshape(rows, width))
    g_low = g.astype(BF)
    gain1, gain2 = gains_ref[0:1, :], gains_ref[1:2, :]

    r1 = lax.rsqrt(jnp.mean(x * x, -1, keepdims=True) + EPS)
    ub = (x * r1 * gain1).astype(BF)
    proj_ref[...] = dot(ub, wqkv_ref[...]).astype(BF)

    own = jnp.where(
        lax.broadcasted_iota(jnp.int32, (wide, width), 0) // zlen
        == lax.broadcasted_iota(jnp.int32, (wide, width), 1) // size, 1.0, 0.0
    ).astype(BF)
    head_of = lax.broadcasted_iota(jnp.int32, (zlen, width), 1) // size
    scale = size ** (-0.5)

    def spread(block):
        return jnp.concatenate([block] * HEADS, axis=0) * own

    def gathered(stack):
        total = stack[:zlen]
        for head in range(1, HEADS):
            total = jnp.where(head_of == head, stack[head * zlen : (head + 1) * zlen], total)
        return total

    def rows_of(ref, pixel, column):
        return ref[pixel * zlen : (pixel + 1) * zlen, column * width : (column + 1) * width]

    for pixel in range(pixels):
        query, keys, values = (rows_of(proj_ref, pixel, i) for i in range(3))
        scores = dot(keys, spread(query), (1, 1)) * scale
        raised = jnp.exp(scores - jnp.max(scores, 0, keepdims=True))
        probs = raised * (1.0 / jnp.sum(raised, 0, keepdims=True))
        probs_ref[pixel] = probs
        mixed_ref[pixel * zlen : (pixel + 1) * zlen, :] = gathered(
            dot(probs.astype(BF), values, (0, 0))
        ).astype(BF)

    mixed = mixed_ref[...]
    h = x + dot(mixed, wout_ref[...]).astype(BF).astype(F32)
    r2 = lax.rsqrt(jnp.mean(h * h, -1, keepdims=True) + EPS)
    wb = (h * r2 * gain2).astype(BF)
    pre = dot(wb, wup_ref[...])
    act = jax.nn.sigmoid(pre)
    mb = (pre * act).astype(BF)
    g_down = dot(mb, g_low, (0, 0))
    dmb = dot(g_low, wdown_ref[...], (1, 1))
    dpre = (dmb * act * (1.0 + pre * (1.0 - act))).astype(BF)
    g_up = dot(wb, dpre, (0, 0))
    gd = dot(dpre, wup_ref[...], (1, 1)) * gain2
    dh_low = (g + (r2 * gd - h * (r2 * r2 * r2) * jnp.mean(gd * h, -1, keepdims=True))).astype(BF)
    g_out = dot(mixed, dh_low, (0, 0))
    dmixed_ref[...] = dot(dh_low, wout_ref[...], (1, 1)).astype(BF)

    for pixel in range(pixels):
        query, keys, values = (rows_of(proj_ref, pixel, i) for i in range(3))
        spread_grad = spread(rows_of(dmixed_ref, pixel, 0))
        probs = probs_ref[pixel]
        dprobs = dot(values, spread_grad, (1, 1))
        dvalues = dot(probs.astype(BF), spread_grad)
        dscores = (
            probs * (dprobs - jnp.sum(probs * dprobs, 0, keepdims=True)) * scale
        ).astype(BF)
        dkeys = dot(dscores, spread(query))
        dquery = gathered(dot(dscores, keys, (0, 0)))
        here = slice(pixel * zlen, (pixel + 1) * zlen)
        dproj_ref[here, :width] = dquery.astype(BF)
        dproj_ref[here, width : 2 * width] = dkeys.astype(BF)
        dproj_ref[here, 2 * width :] = dvalues.astype(BF)

    dproj = dproj_ref[...]
    g_qkv = dot(ub, dproj, (0, 0))
    ge = dot(dproj, wqkv_ref[...], (1, 1)) * gain1
    dxa = (r1 * ge - x * (r1 * r1 * r1) * jnp.mean(ge * x, -1, keepdims=True)).astype(BF)
    dx = (dh_low.astype(F32) + dxa.astype(F32)).astype(BF)
    dx_ref[...] = dot(order, dx, (0, 0)).astype(BF).reshape(dx_ref.shape)

    def columns(out, start, block):
        tall = block.shape[0]
        for i in range(block.shape[1] // LANES):
            out[start + i * tall : start + (i + 1) * tall, :] = block[
                :, i * LANES : (i + 1) * LANES
            ].astype(BF)
        return start + tall * (block.shape[1] // LANES)

    def fill(attention, mlp):
        columns(attention, columns(attention, 0, g_qkv), g_out)
        columns(mlp, columns(mlp, 0, g_up), g_down)

    @pl.when(core_ref[0] == 0)
    def _():
        fill(keep_ref, send_ref)

    @pl.when(core_ref[0] != 0)
    def _():
        fill(send_ref, keep_ref)


def sum_kernel(copies, in_ref, out_ref):
    total = in_ref[0].astype(F32)
    for i in range(1, in_ref.shape[0]):
        total += in_ref[i].astype(F32)
    low = total.astype(BF)
    for i in range(copies):
        out_ref[i] = low


def pair_kernel(mine_ref, other_ref, out_ref):
    out_ref[...] = (mine_ref[...].astype(F32) + other_ref[...].astype(F32)).astype(BF)


def finish_kernel(
    factor, core_ref, mine_ref, other_ref, wqkv_ref, wup_ref, gains_ref,
    qkv_ref, out_ref, up_ref, down_ref, ggains_ref,
):
    def columns(half, start, ref):
        tall = ref.shape[0]
        for i in range(ref.shape[1] // LANES):
            ref[:, i * LANES : (i + 1) * LANES] = (
                half[start + i * tall : start + (i + 1) * tall, :].astype(F32) * factor
            )
        return start + tall * (ref.shape[1] // LANES)

    def split(attention, mlp):
        columns(attention, columns(attention, 0, qkv_ref), out_ref)
        columns(mlp, columns(mlp, 0, up_ref), down_ref)

    @pl.when(core_ref[0] == 0)
    def _():
        split(mine_ref, other_ref)

    @pl.when(core_ref[0] != 0)
    def _():
        split(other_ref, mine_ref)

    one = jnp.sum(wqkv_ref[...].astype(F32) * qkv_ref[...], -1)
    two = jnp.sum(wup_ref[...].astype(F32) * up_ref[...], -1)
    ggains_ref[...] = jnp.stack([one, two]) / gains_ref[...]


def call(kernel, outs, args, scratch=(), core=False, cost=None):
    specs = [pl.BlockSpec(memory_space=pltpu.VMEM)] * len(args)
    if core:
        specs[0] = pl.BlockSpec(memory_space=pltpu.SMEM)
    single = not isinstance(outs, (list, tuple))
    return pl.pallas_call(
        kernel,
        out_shape=outs,
        in_specs=specs,
        out_specs=pl.BlockSpec(memory_space=pltpu.VMEM)
        if single
        else [pl.BlockSpec(memory_space=pltpu.VMEM)] * len(outs),
        scratch_shapes=list(scratch),
        compiler_params=pltpu.CompilerParams(vmem_limit_bytes=VMEM_LIMIT),
    )(*args)


def shape(dims, kind=BF):
    return jax.ShapeDtypeStruct(tuple(dims), kind)


def body(features, grad_output, qkv_weight, out_weight, up_weight, down_weight, norm_gains):
    sections, pixels, width = features.shape
    peers = lax.axis_size(("x", "h", "c"))
    near = pixels // peers
    hidden = up_weight.shape[1]
    core = lax.axis_index("c").astype(jnp.int32).reshape(1)

    def by_peer(a):
        return a.reshape(sections, peers, near, width).transpose(1, 0, 2, 3).reshape(peers, sections * near, width)

    both = jnp.concatenate([by_peer(features), by_peer(grad_output)], axis=1)
    xg = lax.all_to_all(both, ("x", "h", "c"), split_axis=0, concat_axis=0, tiled=True)
    rows = peers * sections * near
    zlen = peers * sections
    pack = (width * 4 * width) // LANES
    dx, send, keep = call(
        functools.partial(block_kernel, near),
        [shape((peers, sections * near, width)), shape((pack, LANES)), shape((pack, LANES))],
        (core, xg, qkv_weight, out_weight, up_weight, down_weight, norm_gains),
        scratch=[
            pltpu.VMEM((rows, 3 * width), BF),
            pltpu.VMEM((near, zlen, HEADS * zlen), F32),
            pltpu.VMEM((rows, width), BF),
            pltpu.VMEM((rows, width), BF),
            pltpu.VMEM((rows, 3 * width), BF),
        ],
        core=True,
    )
    back = lax.all_to_all(dx, ("x", "h", "c"), split_axis=0, concat_axis=0, tiled=True)
    input_grad = back.reshape(peers, sections, near, width).transpose(1, 0, 2, 3).reshape(features.shape)

    swap = [(0, 1), (1, 0)]
    other = lax.ppermute(send, "c", swap)
    pair = call(pair_kernel, shape((pack, LANES)), (keep, other))
    plane, line = lax.axis_size(("y", "x")), lax.axis_size(("l", "h"))
    own = pack // plane
    parts = lax.all_to_all(pair.reshape(plane, own, LANES), ("y", "x"), split_axis=0, concat_axis=0, tiled=True)
    copies = call(functools.partial(sum_kernel, line), shape((line, own, LANES)), (parts,))
    parts = lax.all_to_all(copies, ("l", "h"), split_axis=0, concat_axis=0, tiled=True)
    copies = call(functools.partial(sum_kernel, plane), shape((plane, own, LANES)), (parts,))
    mine = lax.all_to_all(copies, ("y", "x"), split_axis=0, concat_axis=0, tiled=True).reshape(pack, LANES)
    other = lax.ppermute(mine, "c", swap)
    voxels = sections * peers * pixels * lax.axis_size(("y", "l"))
    grads = call(
        functools.partial(finish_kernel, float(voxels) ** (-0.5)),
        [
            shape((width, 3 * width), F32),
            shape((width, width), F32),
            shape((width, hidden), F32),
            shape((hidden, width), F32),
            shape((2, width), F32),
        ],
        (core, mine, other, qkv_weight, up_weight, norm_gains),
        core=True,
    )
    return (input_grad, *grads)


def solution(mesh):
    fine = Mesh(mesh.devices.reshape(8, 2, 4, 4, 2), ("y", "l", "x", "h", "c"))
    big = P(("x", "h", "c"), ("y", "l"), None)
    in_specs = (big, big, P(), P(), P(), P(), P())
    out_specs = (big, P(), P(), P(), P(), P())
    return jax.shard_map(body, mesh=fine, in_specs=in_specs, out_specs=out_specs, check_vma=False)
```

time: 419 us -> 141 us (0.34)
  waiting for transfers between devices: 205 us -> 30.3 us
  blocking collectives: 101 us -> 57 us
  matrix products: 28.4 us -> 0 us
  local copies, waits for them, and re-layouts: 30 us -> 5.03 us
  Pallas kernels: 0 us -> 18.4 us
  between operations: 14.5 us -> 0.69 us
  other arithmetic: 12.6 us -> 0.86 us
    psum x1 -> x0, waiting for transfers between devices: 169 us -> none  [body(): lax.psum((g_qkv, g_out, g_up, g_down, g_gains), ('grp', 'gz'))]
    psum x1 -> x0, blocking collectives: 101 us -> none  [body(): lax.psum((g_qkv, g_out, g_up, g_down, g_gains), ('grp', 'gz'))]
    all_to_all x0 -> x3, blocking collectives: none -> 57 us  [the longest x1 26.4 us: body(): lax.all_to_all(pair.reshape(plane, own, LANES), ('y', 'x'), split_axis=0,...]
    dot_general x16 -> x0, matrix products: 26.2 us -> none  [mix(): return jnp.einsum(form, left, right, preferred_element_type=jnp.float32)]
    pallas_call x0 -> x5, Pallas kernels: none -> 18.4 us  [call(): pl.pallas_call(kernel, out_shape=outs, in_specs=specs, out_specs=pl.Block...]
    reshape x6 -> x2, local copies, waits for them, and re-layouts: 9.7 us -> 1.7 us  [the longest x1 0.98 us: by_peer(): a.reshape(sections, peers, near, width).transpose(1, 0, 2, 3)]
    all_to_all x4 -> x2, waiting for transfers between devices: 35.2 us -> 28.6 us  [the longest x1 17.2 us: body(): lax.all_to_all(both, ('x', 'h', 'c'), split_axis=0, concat_axis=0, tiled=...]
    unnamed x59 -> x10, local copies, waits for them, and re-layouts: 9.67 us -> 3.33 us
  transfers between devices with their start and end apart: 5 -> 4, of which waited for: 4 -> 3; matrix products, arithmetic and copies ran while one was open for 2% -> 1% of each run, Pallas kernels for 0% -> 0%
where the time goes in v1:
time: 141 us
  blocking collectives  57 us (40%)
  waiting for transfers between devices  30.3 us (21%)
  starting transfers between devices  28.4 us (20%)
  Pallas kernels  18.4 us (13%)
  local copies, waits for them, and re-layouts  5.03 us (4%)
    all_to_all x1, blocking collectives, body(): lax.all_to_all(pair.reshape(plane, own, LANES), ('y', 'x'), split_axis=0,...  26.4 us
    all_to_all x1, blocking collectives, body(): lax.all_to_all(copies, ('y', 'x'), split_axis=0, concat_axis=0, tiled=True)  19.5 us
    pallas_call x5, Pallas kernels, call(): pl.pallas_call(kernel, out_shape=outs, in_specs=specs, out_specs=pl.Block...  18.4 us
    all_to_all x1, waiting for transfers between devices, body(): lax.all_to_all(both, ('x', 'h', 'c'), split_axis=0, concat_axis=0, tiled=...  17.2 us
    all_to_all x1, starting transfers between devices, body(): lax.all_to_all(both, ('x', 'h', 'c'), split_axis=0, concat_axis=0, tiled=...  14.4 us
    all_to_all x1, waiting for transfers between devices, body(): lax.all_to_all(dx, ('x', 'h', 'c'), split_axis=0, concat_axis=0, tiled=True)  11.3 us
    all_to_all x1, blocking collectives, body(): lax.all_to_all(copies, ('l', 'h'), split_axis=0, concat_axis=0, tiled=True)  11 us
    all_to_all x1, starting transfers between devices, body(): lax.all_to_all(dx, ('x', 'h', 'c'), split_axis=0, concat_axis=0, tiled=True)  9.17 us
  transfers between devices with their start and end apart: 4, of which 3 were waited for; matrix products, arithmetic and copies ran while one was open for 1% of the time, Pallas kernels for 0%

profile of v1, /device:TPU:1, one launch (start us, length us, event | category | flops | bytes accessed | tf_op | source)
XLA Modules:
  0.0 140.6 jit_solution(12221222256166736263)
XLA Ops:
  0.6 0.0 copy-start
  0.6 0.9 copy-done
  1.6 1.0 copy_bitcast_fusion.1
  2.6 0.9 pad_maximum_fusion
  3.4 14.4 %all-to-all-start = ((bf16[32,32,256]{2,1,0:T(8,128)(2,1)}), bf16[32,32,256]{2,1,0:T(8,128)(2,1)S(1)}, u32[]{:S(2)}, u32[]{:S(2)}) async-start(bf16[32,32,256]{2,1,0:T(8,128)(2,1)} %pad_maximum_fusion), calls=%async_computation | async-start | bytes 1048576 | tf_op jit(solution)/shard_map/all_to_all | solution.py:211
  17.9 17.2 %all-to-all-done.xg_ref = bf16[32,32,256]{2,1,0:T(8,128)(2,1)S(1)} async-done(((bf16[32,32,256]{2,1,0:T(8,128)(2,1)}), bf16[32,32,256]{2,1,0:T(8,128)(2,1)S(1)}, u32[]{:S(2)}, u32[]{:S(2)}) %all-to-all-start) | async-done | bytes 524320 | tf_op jit(solution)/shard_map/all_to_all | solution.py:211
  35.1 0.8 copy-done.2
  35.9 9.9 %shard_map.118 = (bf16[32,16,256]{2,1,0:T(8,128)(2,1)}, bf16[2048,128]{1,0:T(8,128)(2,1)}, bf16[2048,128]{1,0:T(8,128)(2,1)}) custom-call(s32[1]{0:T(128)} %bitcast.core_ref, bf16[32,32,256]{2,1,0:T(8,128)(2,1)} %copy-done.2, bf16[256,768]{1,0:T(8,128)(2,1)} %wqkv_ref.3, bf16[256,256]{1,0:T(8,128)(2,1)} %wout_ref.1, bf16[256,512]{1,0:T(8,128)(2,1)} %wup_ref.3, ...), custom_call_target="tpu_custom_call" | custom-call | tf_op jit(solution)/shard_map/pallas_call | solution.py:184
  45.8 2.6 %collective-permute-start = (bf16[2048,128]{1,0:T(8,128)(2,1)}, bf16[2048,128]{1,0:T(8,128)(2,1)S(1)}, u32[]{:S(2)}, u32[]{:S(2)}) collective-permute-start(bf16[2048,128]{1,0:T(8,128)(2,1)} %get-tuple-element.16), channel_id=1, source_target_pairs={{0,1},{1,0},{2,3},{3,2},{4,5},{5,4},{6,7},{7,6},{8,9},{9,8},{10,11... | collective-permute-start | bytes 1572872 | tf_op jit(solution)/shard_map/ppermute | solution.py:232
  48.4 1.7 %collective-permute-done.other_ref = bf16[2048,128]{1,0:T(8,128)(2,1)S(1)} collective-permute-done((bf16[2048,128]{1,0:T(8,128)(2,1)}, bf16[2048,128]{1,0:T(8,128)(2,1)S(1)}, u32[]{:S(2)}, u32[]{:S(2)}) %collective-permute-start) | collective-permute-done | bytes 524320 | tf_op jit(solution)/shard_map/ppermute | solution.py:232
  50.2 0.8 copy-done.4
  50.9 2.1 %shard_map.119 = bf16[2048,128]{1,0:T(8,128)(2,1)} custom-call(bf16[2048,128]{1,0:T(8,128)(2,1)} %get-tuple-element.15.mine_ref, bf16[2048,128]{1,0:T(8,128)(2,1)} %copy-done.4), custom_call_target="tpu_custom_call" | custom-call | tf_op jit(solution)/shard_map/pallas_call | solution.py:184
  53.1 26.4 %all_to_all.25.in_ref = bf16[32,64,128]{2,1,0:T(8,128)(2,1)} all-to-all(bf16[32,64,128]{2,1,0:T(8,128)(2,1)} %bitcast.26), channel_id=1, replica_groups=mesh['y'=8,'l'=2,'x'=4,'h'=4,'c'=2] {'y','x'}, dimensions={0} | all-to-all | bytes 1048576 | tf_op jit(solution)/shard_map/all_to_all | solution.py:236
  79.5 1.8 %shard_map.120 = bf16[8,64,128]{2,1,0:T(8,128)(2,1)} custom-call(bf16[32,64,128]{2,1,0:T(8,128)(2,1)} %all_to_all.25.in_ref), custom_call_target="tpu_custom_call" | custom-call | tf_op jit(solution)/shard_map/pallas_call | solution.py:184
  81.3 11.0 %all_to_all.26.in_ref = bf16[8,64,128]{2,1,0:T(8,128)(2,1)} all-to-all(bf16[8,64,128]{2,1,0:T(8,128)(2,1)} %shard_map.120), channel_id=1, replica_groups=mesh['y'=8,'l'=2,'x'=4,'h'=4,'c'=2] {'l','h'}, dimensions={0} | all-to-all | bytes 262144 | tf_op jit(solution)/shard_map/all_to_all | solution.py:238
  92.3 1.8 %shard_map.121 = bf16[32,64,128]{2,1,0:T(8,128)(2,1)} custom-call(bf16[8,64,128]{2,1,0:T(8,128)(2,1)} %all_to_all.26.in_ref), custom_call_target="tpu_custom_call" | custom-call | tf_op jit(solution)/shard_map/pallas_call | solution.py:184
  94.1 19.5 %all_to_all.27 = bf16[32,64,128]{2,1,0:T(8,128)(2,1)S(1)} all-to-all(bf16[32,64,128]{2,1,0:T(8,128)(2,1)} %shard_map.121), channel_id=1, replica_groups=mesh['y'=8,'l'=2,'x'=4,'h'=4,'c'=2] {'y','x'}, dimensions={0} | all-to-all | bytes 1048576 | tf_op jit(solution)/shard_map/all_to_all | solution.py:240
  113.6 9.2 %all-to-all-start.1 = ((bf16[32,16,256]{2,1,0:T(8,128)(2,1)}), bf16[32,16,256]{2,1,0:T(8,128)(2,1)S(1)}, u32[]{:S(2)}, u32[]{:S(2)}) async-start(bf16[32,16,256]{2,1,0:T(8,128)(2,1)} %get-tuple-element.14), calls=%async_computation.1 | async-start | bytes 524288 | tf_op jit(solution)/shard_map/all_to_all | solution.py:228
  122.8 2.1 %collective-permute-start.1 = (bf16[2048,128]{1,0:T(8,128)(2,1)S(1)}, bf16[2048,128]{1,0:T(8,128)(2,1)S(1)}, u32[]{:S(2)}, u32[]{:S(2)}) collective-permute-start(bf16[2048,128]{1,0:T(8,128)(2,1)S(1)} %bitcast.24), channel_id=1, source_target_pairs={{0,1},{1,0},{2,3},{3,2},{4,5},{5,4},{6,7},{7,6},{8,9},{9,8},{10,11... | collective-permute-start | bytes 1572872 | tf_op jit(solution)/shard_map/ppermute | solution.py:241
  124.9 11.3 %all-to-all-done.1 = bf16[32,16,256]{2,1,0:T(8,128)(2,1)S(1)} async-done(((bf16[32,16,256]{2,1,0:T(8,128)(2,1)}), bf16[32,16,256]{2,1,0:T(8,128)(2,1)S(1)}, u32[]{:S(2)}, u32[]{:S(2)}) %all-to-all-start.1) | async-done | bytes 262176 | tf_op jit(solution)/shard_map/all_to_all | solution.py:228
  136.3 0.7 copy_bitcast_fusion
  137.0 0.0 collective-permute-done.1.other_ref
  137.0 0.8 copy-done.3
  137.8 2.9 %shard_map.122 = (f32[256,768]{1,0:T(8,128)}, f32[256,256]{1,0:T(8,128)}, f32[256,512]{1,0:T(8,128)}, f32[512,256]{1,0:T(8,128)}, f32[2,256]{1,0:T(2,128)}) custom-call(s32[1]{0:T(128)} %bitcast.core_ref, bf16[2048,128]{1,0:T(8,128)(2,1)} %bitcast.25, bf16[2048,128]{1,0:T(8,128)(2,1)} %copy-done.3, bf16[256,768]{1,0:T(8,128)(2,1)} %wqkv_ref.3, ...), custom_call_target="tpu_custom_call" | custom-call | tf_op jit(solution)/shard_map/pallas_call | solution.py:184
  (5 shorter events, 0.0 us)
Async XLA Ops:
  0.6 1.0 copy-start
  3.4 31.7 %all-to-all-start = ((bf16[32,32,256]{2,1,0:T(8,128)(2,1)}), bf16[32,32,256]{2,1,0:T(8,128)(2,1)S(1)}, u32[]{:S(2)}, u32[]{:S(2)}) async-start(bf16[32,32,256]{2,1,0:T(8,128)(2,1)} %pad_maximum_fusion), calls=%async_computation | async-start | bytes 1048576 | tf_op jit(solution)/shard_map/all_to_all | solution.py:211
  35.1 0.8 copy-start.2
  45.8 4.4 %collective-permute-start = (bf16[2048,128]{1,0:T(8,128)(2,1)}, bf16[2048,128]{1,0:T(8,128)(2,1)S(1)}, u32[]{:S(2)}, u32[]{:S(2)}) collective-permute-start(bf16[2048,128]{1,0:T(8,128)(2,1)} %get-tuple-element.16), channel_id=1, source_target_pairs={{0,1},{1,0},{2,3},{3,2},{4,5},{5,4},{6,7},{7,6},{8,9},{9,8},{10,11... | collective-permute-start | bytes 1572872 | tf_op jit(solution)/shard_map/ppermute | solution.py:232
  50.1 0.8 copy-start.4
  113.6 23.4 %copy-start.1 = (bf16[32,64,128]{2,1,0:T(8,128)(2,1)}, bf16[32,64,128]{2,1,0:T(8,128)(2,1)S(1)}, u32[]{:S(2)}) copy-start(bf16[32,64,128]{2,1,0:T(8,128)(2,1)S(1)} %all_to_all.27) | copy-start | bytes 1572868
  113.6 22.7 %all-to-all-start.1 = ((bf16[32,16,256]{2,1,0:T(8,128)(2,1)}), bf16[32,16,256]{2,1,0:T(8,128)(2,1)S(1)}, u32[]{:S(2)}, u32[]{:S(2)}) async-start(bf16[32,16,256]{2,1,0:T(8,128)(2,1)} %get-tuple-element.14), calls=%async_computation.1 | async-start | bytes 524288 | tf_op jit(solution)/shard_map/all_to_all | solution.py:228
  122.8 14.2 %collective-permute-start.1 = (bf16[2048,128]{1,0:T(8,128)(2,1)S(1)}, bf16[2048,128]{1,0:T(8,128)(2,1)S(1)}, u32[]{:S(2)}, u32[]{:S(2)}) collective-permute-start(bf16[2048,128]{1,0:T(8,128)(2,1)S(1)} %bitcast.24), channel_id=1, source_target_pairs={{0,1},{1,0},{2,3},{3,2},{4,5},{5,4},{6,7},{7,6},{8,9},{9,8},{10,11... | collective-permute-start | bytes 1572872 | tf_op jit(solution)/shard_map/ppermute | solution.py:241
  137.0 0.8 copy-start.3

commit v2 on v1

v2 whole, which is shorter than its diff:
```python
import functools
import itertools

import jax
import jax.numpy as jnp
from jax import lax
from jax.experimental import pallas as pl
from jax.experimental.pallas import tpu as pltpu
from jax.sharding import Mesh
from jax.sharding import PartitionSpec as P

HEADS = 8
EPS = 1e-06
BF, F32 = jnp.bfloat16, jnp.float32
LANES = 128
AXES = ("y", "l", "x", "h", "c")
MIB = 1024 * 1024


def dot(left, right, over=(1, 0)):
    return lax.dot_general(
        left, right, (((over[0],), (over[1],)), ((), ())), preferred_element_type=F32
    )


def lanes(out, start, block):
    tall = block.shape[-2]
    for i in range(block.shape[-1] // LANES):
        rows = slice(start + i * tall, start + (i + 1) * tall)
        out[..., rows, :] = block[..., i * LANES : (i + 1) * LANES].astype(BF)
    return start + tall * (block.shape[-1] // LANES)


def block_kernel(
    pixels, xg_ref, wqkv_ref, wout_ref, wup_ref, wdown_ref, gains_ref,
    dx_ref, ub_ref, dproj_ref, mixed_ref, dh_ref, wb_ref, dpre_ref, mb_ref, g_ref,
    proj_ref, probs_ref, dmixed_ref,
):
    sources, both, width = xg_ref.shape
    half = both // 2
    rows = sources * half
    zlen = rows // pixels
    size = width // HEADS
    wide = HEADS * zlen
    hidden_units = wup_ref.shape[1]

    at = lax.broadcasted_iota(jnp.int32, (rows, rows), 0)
    to = lax.broadcasted_iota(jnp.int32, (rows, rows), 1)
    order = jnp.where(to == (at % zlen) * pixels + at // zlen, 1.0, 0.0).astype(BF)
    x = dot(order, xg_ref[:, :half, :].reshape(rows, width))
    g = dot(order, xg_ref[:, half:, :].reshape(rows, width))
    g_low = g.astype(BF)
    g_ref[...] = g_low
    gain1, gain2 = gains_ref[0:1, :], gains_ref[1:2, :]

    r1 = lax.rsqrt(jnp.mean(x * x, -1, keepdims=True) + EPS)
    ub = (x * r1 * gain1).astype(BF)
    ub_ref[...] = ub
    proj_ref[...] = dot(ub, wqkv_ref[...]).astype(BF)

    own = jnp.where(
        lax.broadcasted_iota(jnp.int32, (wide, width), 0) // zlen
        == lax.broadcasted_iota(jnp.int32, (wide, width), 1) // size, 1.0, 0.0
    ).astype(BF)
    head_of = lax.broadcasted_iota(jnp.int32, (zlen, width), 1) // size
    scale = size ** (-0.5)

    def spread(block):
        return jnp.concatenate([block] * HEADS, axis=0) * own

    def gathered(stack):
        total = stack[:zlen]
        for head in range(1, HEADS):
            total = jnp.where(head_of == head, stack[head * zlen : (head + 1) * zlen], total)
        return total

    def rows_of(ref, pixel, column):
        return ref[pixel * zlen : (pixel + 1) * zlen, column * width : (column + 1) * width]

    for pixel in range(pixels):
        query, keys, values = (rows_of(proj_ref, pixel, i) for i in range(3))
        scores = dot(keys, spread(query), (1, 1)) * scale
        raised = jnp.exp(scores - jnp.max(scores, 0, keepdims=True))
        probs = raised * (1.0 / jnp.sum(raised, 0, keepdims=True))
        probs_ref[pixel] = probs
        mixed_ref[pixel * zlen : (pixel + 1) * zlen, :] = gathered(
            dot(probs.astype(BF), values, (0, 0))
        ).astype(BF)

    mixed = mixed_ref[...]
    h = x + dot(mixed, wout_ref[...]).astype(BF).astype(F32)
    r2 = lax.rsqrt(jnp.mean(h * h, -1, keepdims=True) + EPS)
    wb = (h * r2 * gain2).astype(BF)
    wb_ref[...] = wb
    pre = dot(wb, wup_ref[...])
    act = jax.nn.sigmoid(pre)
    mb_ref[...] = (pre * act).astype(BF)
    dmb = dot(g_low, wdown_ref[...], (1, 1))
    dpre = (dmb * act * (1.0 + pre * (1.0 - act))).astype(BF)
    dpre_ref[...] = dpre
    gd = dot(dpre, wup_ref[...], (1, 1)) * gain2
    dh_low = (g + (r2 * gd - h * (r2 * r2 * r2) * jnp.mean(gd * h, -1, keepdims=True))).astype(BF)
    dh_ref[...] = dh_low
    dmixed_ref[...] = dot(dh_low, wout_ref[...], (1, 1)).astype(BF)

    for pixel in range(pixels):
        query, keys, values = (rows_of(proj_ref, pixel, i) for i in range(3))
        spread_grad = spread(rows_of(dmixed_ref, pixel, 0))
        probs = probs_ref[pixel]
        dprobs = dot(values, spread_grad, (1, 1))
        dvalues = dot(probs.astype(BF), spread_grad)
        dscores = (
            probs * (dprobs - jnp.sum(probs * dprobs, 0, keepdims=True)) * scale
        ).astype(BF)
        dkeys = dot(dscores, spread(query))
        dquery = gathered(dot(dscores, keys, (0, 0)))
        here = slice(pixel * zlen, (pixel + 1) * zlen)
        dproj_ref[here, :width] = dquery.astype(BF)
        dproj_ref[here, width : 2 * width] = dkeys.astype(BF)
        dproj_ref[here, 2 * width :] = dvalues.astype(BF)

    dproj = dproj_ref[...]
    ge = dot(dproj, wqkv_ref[...], (1, 1)) * gain1
    dxa = (r1 * ge - x * (r1 * r1 * r1) * jnp.mean(ge * x, -1, keepdims=True)).astype(BF)
    dx = (dh_low.astype(F32) + dxa.astype(F32)).astype(BF)
    dx = dot(order, dx, (0, 0)).reshape(sources // 2, 2, half, width)
    lanes(dx_ref, lanes(dx_ref, 0, dx[:, 0]), dx[:, 1])


def weights_kernel(
    place_ref, dx_ref, ub_ref, dproj_ref, mixed_ref, dh_ref, wb_ref, dpre_ref, mb_ref, g_ref, send_ref, keep_ref
):
    def fill(attention, mlp):
        lanes(mlp, lanes(mlp, 0, dot(wb_ref[...], dpre_ref[...], (0, 0))), dot(mb_ref[...], g_ref[...], (0, 0)))
        lanes(
            attention,
            lanes(attention, 0, dot(ub_ref[...], dproj_ref[...], (0, 0))),
            dot(mixed_ref[...], dh_ref[...], (0, 0)),
        )

    pack = keep_ref.shape[0]
    chips, tall = dx_ref.shape[:2]

    @pl.when(place_ref[0] == 0)
    def _():
        fill(keep_ref, send_ref)

    @pl.when(place_ref[0] != 0)
    def _():
        fill(send_ref, keep_ref)
        for chip in range(chips):
            send_ref[pack + chip * tall : pack + (chip + 1) * tall, :] = dx_ref[chip]


def arrange_kernel(x_ref, g_ref, out_ref):
    peers, _, width = out_ref.shape
    parts = [
        ref[z].astype(F32).reshape(peers, -1, width) for ref in (x_ref, g_ref) for z in range(x_ref.shape[0])
    ]
    out_ref[...] = jnp.concatenate(parts, axis=1).astype(BF)


def pair_kernel(place_ref, mine_ref, other_ref, dx_ref, out_ref):
    pack = mine_ref.shape[0]
    chips, tall = dx_ref.shape[:2]
    own = pack // out_ref.shape[0]
    for to in range(out_ref.shape[0]):
        rows = slice(to * own, (to + 1) * own)
        out_ref[to, :own, :] = (mine_ref[rows, :].astype(F32) + other_ref[rows, :].astype(F32)).astype(BF)

    @pl.when(place_ref[0] == 0)
    def _():
        for chip in range(chips):
            out_ref[2 * chip, own:, :] = dx_ref[chip]
            out_ref[2 * chip + 1, own:, :] = other_ref[pack + chip * tall : pack + (chip + 1) * tall, :]


def total_of(ref, rows):
    total = ref[0, :rows, :].astype(F32)
    for i in range(1, ref.shape[0]):
        total += ref[i, :rows, :].astype(F32)
    return total.astype(BF)


def first_sum_kernel(place_ref, in_ref, out_ref, stay_ref, pass_ref):
    own = out_ref.shape[1]
    low = total_of(in_ref, own)
    for i in range(out_ref.shape[0]):
        out_ref[i] = low

    def sort(side):
        for chip in range(stay_ref.shape[0]):
            stay_ref[chip] = in_ref[2 * chip + side, own:, :]
            pass_ref[chip] = in_ref[2 * chip + 1 - side, own:, :]

    @pl.when(place_ref[1] == 0)
    def _():
        sort(0)

    @pl.when(place_ref[1] != 0)
    def _():
        sort(1)


def second_sum_kernel(place_ref, in_ref, stay_ref, passed_ref, out_ref, own_ref, next_ref):
    low = total_of(in_ref, in_ref.shape[1])
    for i in range(out_ref.shape[0]):
        out_ref[i] = low
    chips, tall = stay_ref.shape[0], stay_ref.shape[1] // 2

    def sort(blocks):
        for chip in range(chips):
            for core in range(2):
                at = slice((2 * chip + core) * tall, (2 * chip + core + 1) * tall)
                own_ref[at, :] = blocks[core][chip, :tall, :]
                next_ref[at, :] = blocks[core][chip, tall:, :]

    @pl.when(place_ref[1] == 0)
    def _():
        sort((stay_ref, passed_ref))

    @pl.when(place_ref[1] != 0)
    def _():
        sort((passed_ref, stay_ref))


def join_kernel(mine_ref, next_ref, out_ref):
    pack = mine_ref.shape[0]
    out_ref[:pack, :] = mine_ref[...]
    out_ref[pack:, :] = next_ref[...]


def finish_kernel(
    factor, near, place_ref, mine_ref, other_ref, own_ref, wqkv_ref, wup_ref, gains_ref,
    input_ref, qkv_ref, out_ref, up_ref, down_ref, ggains_ref,
):
    pack = mine_ref.shape[0]
    sections, pixels, width = input_ref.shape
    def columns(half, start, ref):
        tall = ref.shape[0]
        for i in range(ref.shape[1] // LANES):
            ref[:, i * LANES : (i + 1) * LANES] = (
                half[start + i * tall : start + (i + 1) * tall, :].astype(F32) * factor
            )
        return start + tall * (ref.shape[1] // LANES)

    def split(attention, mlp):
        columns(attention, columns(attention, 0, qkv_ref), out_ref)
        columns(mlp, columns(mlp, 0, up_ref), down_ref)

    def arrange(rows):
        blocks = rows.astype(F32).reshape(pixels // near, -1, LANES)
        for i in range(width // LANES):
            for z in range(sections):
                at = (i * sections + z) * near
                input_ref[z, :, i * LANES : (i + 1) * LANES] = (
                    blocks[:, at : at + near, :].reshape(pixels, LANES).astype(BF)
                )

    @pl.when(place_ref[0] == 0)
    def _():
        split(mine_ref, other_ref)
        arrange(own_ref[...])

    @pl.when(place_ref[0] != 0)
    def _():
        split(other_ref, mine_ref)
        arrange(other_ref[pack:, :])

    one = jnp.sum(wqkv_ref[...].astype(F32) * qkv_ref[...], -1)
    two = jnp.sum(wup_ref[...].astype(F32) * up_ref[...], -1)
    ggains_ref[...] = jnp.stack([one, two]) / gains_ref[...]


def call(kernel, outs, args, scratch=(), placed=False, room=6):
    specs = [pl.BlockSpec(memory_space=pltpu.VMEM)] * len(args)
    if placed:
        specs[0] = pl.BlockSpec(memory_space=pltpu.SMEM)
    single = not isinstance(outs, (list, tuple))
    return pl.pallas_call(
        kernel,
        out_shape=outs,
        in_specs=specs,
        out_specs=pl.BlockSpec(memory_space=pltpu.VMEM)
        if single
        else [pl.BlockSpec(memory_space=pltpu.VMEM)] * len(outs),
        scratch_shapes=list(scratch),
        compiler_params=pltpu.CompilerParams(vmem_limit_bytes=room * MIB),
    )(*args)


def shape(dims, kind=BF):
    return jax.ShapeDtypeStruct(tuple(dims), kind)


def groups_of(axes_by_core):
    sizes = [lax.axis_size(axis) for axis in AXES]
    groups = {}
    for core, axes in enumerate(axes_by_core):
        for index in itertools.product(*map(range, sizes)):
            at = dict(zip(AXES, index))
            if at["c"] == core:
                rest = tuple(at[axis] for axis in AXES if axis not in axes)
                groups.setdefault((core, rest), []).append((tuple(at[axis] for axis in axes), index))
    flat = lambda index: functools.reduce(lambda total, pair: total * pair[0] + pair[1], zip(sizes, index), 0)
    return [[flat(index) for _, index in sorted(group)] for group in groups.values()]


def exchange(pieces, groups):
    return lax.all_to_all(
        pieces, AXES, split_axis=0, concat_axis=0, axis_index_groups=groups, tiled=True
    )


def body(features, grad_output, qkv_weight, out_weight, up_weight, down_weight, norm_gains):
    sections, pixels, width = features.shape
    peers = lax.axis_size(("x", "h", "c"))
    near = pixels // peers
    hidden = up_weight.shape[1]
    place = jnp.stack([lax.axis_index("c"), lax.axis_index("l")]).astype(jnp.int32)
    rows = peers * sections * near
    zlen = peers * sections
    pack = (width * 4 * width) // LANES
    chips = peers // 2
    tall = 2 * sections * near * width // LANES
    both = call(arrange_kernel, shape((peers, 2 * sections * near, width)), (features, grad_output))
    xg = lax.all_to_all(both, ("x", "h", "c"), split_axis=0, concat_axis=0, tiled=True)
    wide = [3 * width, width, width, width, hidden, hidden, width]
    dx, *factors = call(
        functools.partial(block_kernel, near),
        [shape((chips, tall, LANES)), shape((rows, width))] + [shape((rows, n)) for n in wide],
        (xg, qkv_weight, out_weight, up_weight, down_weight, norm_gains),
        scratch=[
            pltpu.VMEM((rows, 3 * width), BF),
            pltpu.VMEM((near, zlen, HEADS * zlen), F32),
            pltpu.VMEM((rows, width), BF),
        ],
        room=16,
    )
    send, keep = call(
        weights_kernel,
        [shape((pack + chips * tall, LANES)), shape((pack, LANES))],
        (place, dx, *factors),
        placed=True,
        room=12,
    )
    swap = [(0, 1), (1, 0)]
    other = lax.ppermute(send, "c", swap)
    wide_groups = groups_of((("x", "h", "l"), ("x", "y")))
    line_groups = groups_of((("y",), ("l", "h")))
    slab, line = len(wide_groups[0]), len(line_groups[0])
    own = pack // slab
    pieces = call(pair_kernel, shape((slab, own + tall, LANES)), (place, keep, other, dx), placed=True)
    pieces = exchange(pieces, wide_groups)
    copies, stay, onward = call(
        first_sum_kernel,
        [shape((line, own, LANES))] + [shape((chips, tall, LANES))] * 2,
        (place, pieces),
        placed=True,
    )
    passed = lax.ppermute(onward, "l", swap)
    pieces = exchange(copies, line_groups)
    copies, own_rows, next_rows = call(
        second_sum_kernel,
        [shape((slab, own, LANES))] + [shape((chips * tall, LANES))] * 2,
        (place, pieces, stay, passed),
        placed=True,
    )
    mine = exchange(copies, wide_groups).reshape(pack, LANES)
    joined = call(join_kernel, shape((pack + chips * tall, LANES)), (mine, next_rows))
    other = lax.ppermute(joined, "c", swap)
    voxels = sections * peers * pixels * lax.axis_size(("y", "l"))
    return tuple(call(
        functools.partial(finish_kernel, float(voxels) ** (-0.5), near),
        [
            shape(features.shape),
            shape((width, 3 * width), F32),
            shape((width, width), F32),
            shape((width, hidden), F32),
            shape((hidden, width), F32),
            shape((2, width), F32),
        ],
        (place, mine, other, own_rows, qkv_weight, up_weight, norm_gains),
        placed=True,
    ))


def solution(mesh):
    fine = Mesh(mesh.devices.reshape(8, 2, 4, 4, 2), AXES)
    big = P(("x", "h", "c"), ("y", "l"), None)
    in_specs = (big, big, P(), P(), P(), P(), P())
    out_specs = (big, P(), P(), P(), P(), P())
    return jax.shard_map(body, mesh=fine, in_specs=in_specs, out_specs=out_specs, check_vma=False)
```

time: 141 us -> 117 us (0.83)
  waiting for transfers between devices: 30.3 us -> 20.9 us
  Pallas kernels: 18.4 us -> 13 us
  blocking collectives: 57 us -> 52.8 us
  local copies, waits for them, and re-layouts: 5.03 us -> 1.91 us
  starting transfers between devices: 28.4 us -> 26.8 us
    all_to_all x1 -> x0, waiting for transfers between devices: 11.3 us -> none  [body(): lax.all_to_all(dx, ('x', 'h', 'c'), split_axis=0, concat_axis=0, tiled=True)]
    all_to_all x1 -> x0, starting transfers between devices: 9.17 us -> none  [body(): lax.all_to_all(dx, ('x', 'h', 'c'), split_axis=0, concat_axis=0, tiled=True)]
    ppermute x1 -> x2, starting transfers between devices: 2.14 us -> 9.52 us  [the longest x1 6.62 us: body(): other = lax.ppermute(joined, 'c', swap)]
    pallas_call x5 -> x8, Pallas kernels: 18.4 us -> 13 us  [call(): pl.pallas_call(kernel, out_shape=outs, in_specs=specs, out_specs=pl.Block...]
    all_to_all x3, blocking collectives: 57 us -> 52.8 us  [exchange(): lax.all_to_all(pieces, AXES, split_axis=0, concat_axis=0, axis_index_grou...]
    ppermute x1 -> x2, waiting for transfers between devices: 0.01 us -> 1.89 us  [the longest x1 1.89 us: body(): other = lax.ppermute(joined, 'c', swap)]
    reshape x2 -> x0, local copies, waits for them, and re-layouts: 1.7 us -> none  [the longest x1 0.98 us: by_peer(): a.reshape(sections, peers, near, width).transpose(1, 0, 2, 3)]
    unnamed x10 -> x14, local copies, waits for them, and re-layouts: 3.33 us -> 1.91 us
  transfers between devices with their start and end apart: 4 -> 4, of which waited for: 3 -> 3; matrix products, arithmetic and copies ran while one was open for 1% -> 0% of each run, Pallas kernels for 0% -> 0%
where the time goes in v2:
time: 117 us; the launch traced here: 116 us
  blocking collectives  52.8 us (45%)
  starting transfers between devices  26.8 us (23%)
  waiting for transfers between devices  20.9 us (18%)
  Pallas kernels  13 us (11%)
  local copies, waits for them, and re-layouts  1.91 us (2%)
    all_to_all x3, blocking collectives, exchange(): lax.all_to_all(pieces, AXES, split_axis=0, concat_axis=0, axis_index_grou...  52.8 us
    all_to_all x1, waiting for transfers between devices, body(): lax.all_to_all(both, ('x', 'h', 'c'), split_axis=0, concat_axis=0, tiled=...  17.1 us
    all_to_all x1, starting transfers between devices, body(): lax.all_to_all(both, ('x', 'h', 'c'), split_axis=0, concat_axis=0, tiled=...  14.6 us
    pallas_call x8, Pallas kernels, call(): pl.pallas_call(kernel, out_shape=outs, in_specs=specs, out_specs=pl.Block...  13 us
    ppermute x1, starting transfers between devices, body(): other = lax.ppermute(joined, 'c', swap)  6.62 us
    ppermute x1, starting transfers between devices, body(): passed = lax.ppermute(onward, 'l', swap)  2.9 us
    ppermute x1, starting transfers between devices, body(): other = lax.ppermute(send, 'c', swap)  2.69 us
  transfers between devices with their start and end apart: 4, of which 3 were waited for; matrix products, arithmetic and copies ran while one was open for 0% of the time, Pallas kernels for 0%

profile of v2, /device:TPU:1, one launch (start us, length us, event | category | flops | bytes accessed | tf_op | source)
XLA Modules:
  0.0 116.2 jit_solution(15836636711559400178)
XLA Ops:
  0.6 0.9 copy-done.2
  1.6 0.9 copy-done.3
  2.5 0.8 shard_map.118
  3.4 14.6 %all-to-all-start = ((bf16[32,32,256]{2,1,0:T(8,128)(2,1)}), bf16[32,32,256]{2,1,0:T(8,128)(2,1)S(1)}, u32[]{:S(2)}, u32[]{:S(2)}) async-start(bf16[32,32,256]{2,1,0:T(8,128)(2,1)} %shard_map.118), calls=%async_computation | async-start | bytes 1048576 | tf_op jit(solution)/shard_map/all_to_all | solution.py:327
  17.9 0.0 copy-start.6
  18.0 0.1 pad_add_fusion.place_ref
  18.0 17.1 %all-to-all-done.xg_ref = bf16[32,32,256]{2,1,0:T(8,128)(2,1)S(1)} async-done(((bf16[32,32,256]{2,1,0:T(8,128)(2,1)}), bf16[32,32,256]{2,1,0:T(8,128)(2,1)S(1)}, u32[]{:S(2)}, u32[]{:S(2)}) %all-to-all-start) | async-done | bytes 524320 | tf_op jit(solution)/shard_map/all_to_all | solution.py:327
  35.2 0.0 copy-done
  35.2 6.7 %shard_map.119 = (bf16[16,64,128]{2,1,0:T(8,128)(2,1)S(1)}, bf16[512,256]{1,0:T(8,128)(2,1)S(1)}, bf16[512,768]{1,0:T(8,128)(2,1)S(1)}, bf16[512,256]{1,0:T(8,12...) custom-call(bf16[32,32,256]{2,1,0:T(8,128)(2,1)S(1)} %all-to-all-don, ...), custom_call_target="tpu_custom_call" | custom-call | tf_op jit(solution)/shard_map/pallas_call | solution.py:280
  41.9 1.3 %shard_map.120 = (bf16[3072,128]{1,0:T(8,128)(2,1)S(1)}, bf16[2048,128]{1,0:T(8,128)(2,1)S(1)}) custom-call(s32[2]{0:T(128)S(1)} %pad_add_fusion.place_ref, bf16[16,64,128]{2,1,0:T(8,128)(2,1)S(1)} %get-tuple-element.23.dx_ref, bf16[512,256]{1,0:T(8,128)(2,1)S(1)} %get-tuple-element.24.ub_ref, bf16[512,768]{1,0:T(8,128)(2,1)S(1)} %get-tuple-element.25.dproj_ref, ...), custom_call_target="tpu_custom_call" | custom-call | tf_op jit(solution)/shard_map/pallas_call | solution.py:280
  43.2 2.7 %collective-permute-start = (bf16[3072,128]{1,0:T(8,128)(2,1)S(1)}, bf16[3072,128]{1,0:T(8,128)(2,1)S(1)}, u32[]{:S(2)}, u32[]{:S(2)}) collective-permute-start(bf16[3072,128]{1,0:T(8,128)(2,1)S(1)} %get-tuple-element.33), channel_id=1, source_target_pairs={{0,1},{1,0},{2,3},{3,2},{4,5},{5,4},{6,7},{7,6},{8,9},{9,8},{10,11... | collective-permute-start | bytes 2359304 | tf_op jit(solution)/shard_map/ppermute | solution.py:348
  45.9 1.9 %collective-permute-done.other_ref = bf16[3072,128]{1,0:T(8,128)(2,1)S(1)} collective-permute-done((bf16[3072,128]{1,0:T(8,128)(2,1)S(1)}, bf16[3072,128]{1,0:T(8,128)(2,1)S(1)}, u32[]{:S(2)}, u32[]{:S(2)}) %collective-permute-start) | collective-permute-done | bytes 786464 | tf_op jit(solution)/shard_map/ppermute | solution.py:348
  47.8 0.7 shard_map.121
  48.5 26.3 %all_to_all.20.in_ref = bf16[32,128,128]{2,1,0:T(8,128)(2,1)S(1)} all-to-all(bf16[32,128,128]{2,1,0:T(8,128)(2,1)S(1)} %shard_map.121), channel_id=1, replica_groups={{0,32,2,34,4,36,6,38,8,40,10,42,12,44,14,46,16,48,18,50,20,52,22,54,24,..., dimensions={0} | all-to-all | bytes 2097152 | tf_op jit(solution)/shard_map/all_to_all | solution.py:310
  74.8 0.6 shard_map.122
  75.5 2.9 %collective-permute-start.1 = (bf16[16,64,128]{2,1,0:T(8,128)(2,1)S(1)}, bf16[16,64,128]{2,1,0:T(8,128)(2,1)S(1)}, u32[]{:S(2)}, u32[]{:S(2)}) collective-permute-start(bf16[16,64,128]{2,1,0:T(8,128)(2,1)S(1)} %get-tuple-element.36), channel_id=1, source_target_pairs={{0,32},{32,0},{1,33},{33,1},{2,34},{34,2},{3,35},{35,3},{4,36},{36... | collective-permute-start | bytes 786440 | tf_op jit(solution)/shard_map/ppermute | solution.py:361
  78.4 9.3 %all_to_all.21.in_ref = bf16[8,64,128]{2,1,0:T(8,128)(2,1)S(1)} all-to-all(bf16[8,64,128]{2,1,0:T(8,128)(2,1)S(1)} %get-tuple-element.34), channel_id=1, replica_groups={{0,64,128,192,256,320,384,448},{2,66,130,194,258,322,386,450},{4,68,132..., dimensions={0} | all-to-all | bytes 262144 | tf_op jit(solution)/shard_map/all_to_all | solution.py:310
  87.6 0.0 collective-permute-done.1.passed_ref
  87.6 0.6 shard_map.123
  88.3 17.2 %all_to_all.22 = bf16[32,64,128]{2,1,0:T(8,128)(2,1)S(1)} all-to-all(bf16[32,64,128]{2,1,0:T(8,128)(2,1)S(1)} %get-tuple-element.37), channel_id=1, replica_groups={{0,32,2,34,4,36,6,38,8,40,10,42,12,44,14,46,16,48,18,50,20,52,22,54,24,..., dimensions={0} | all-to-all | bytes 1048576 | tf_op jit(solution)/shard_map/all_to_all | solution.py:310
  105.5 0.1 shard_map.124
  105.5 6.6 %collective-permute-start.2 = (bf16[3072,128]{1,0:T(8,128)(2,1)S(1)}, bf16[3072,128]{1,0:T(8,128)(2,1)S(1)}, u32[]{:S(2)}, u32[]{:S(2)}) collective-permute-start(bf16[3072,128]{1,0:T(8,128)(2,1)S(1)} %shard_map.124), channel_id=1, source_target_pairs={{0,1},{1,0},{2,3},{3,2},{4,5},{5,4},{6,7},{7,6},{8,9},{9,8},{10,11... | collective-permute-start | bytes 2359304 | tf_op jit(solution)/shard_map/ppermute | solution.py:371
  112.2 1.9 %collective-permute-done.2.other_ref = bf16[3072,128]{1,0:T(8,128)(2,1)S(1)} collective-permute-done((bf16[3072,128]{1,0:T(8,128)(2,1)S(1)}, bf16[3072,128]{1,0:T(8,128)(2,1)S(1)}, u32[]{:S(2)}, u32[]{:S(2)}) %collective-permute-start.2) | collective-permute-done | bytes 786464 | tf_op jit(solution)/shard_map/ppermute | solution.py:371
  114.1 2.2 %shard_map.125 = (bf16[2,256,256]{2,1,0:T(8,128)(2,1)}, f32[256,768]{1,0:T(8,128)}, f32[256,256]{1,0:T(8,128)}, f32[256,512]{1,0:T(8,128)}, f32[512,256]{1,0:T(8,128)}, /*index=5*/f32[2,256]{1,0:T(2,128)}) custom-call(s32[2]{0:T(128)S(1)} %pad_add_fusion.place_ref, bf16[2048,128]{1,0:T(8,128)(2,1)S(1)} %bitcast.4, ...), custom_call_target="tpu_custom_call" | custom-call | tf_op jit(solution)/shard_map/pallas_call | solution.py:280
  (10 shorter events, 0.0 us)
Async XLA Ops:
  0.6 1.0 copy-start.2
  1.6 0.9 copy-start.3
  3.4 31.8 %copy-start = (bf16[256,768]{1,0:T(8,128)(2,1)S(1)}, bf16[256,768]{1,0:T(8,128)(2,1)}, u32[]{:S(2)}) copy-start(bf16[256,768]{1,0:T(8,128)(2,1)} %wqkv_ref.3) | copy-start | bytes 1179652
  3.4 31.8 %copy-start.1 = (bf16[256,512]{1,0:T(8,128)(2,1)S(1)}, bf16[256,512]{1,0:T(8,128)(2,1)}, u32[]{:S(2)}) copy-start(bf16[256,512]{1,0:T(8,128)(2,1)} %wup_ref.3) | copy-start | bytes 786436
  3.4 31.8 %copy-start.4 = (bf16[512,256]{1,0:T(8,128)(2,1)S(1)}, bf16[512,256]{1,0:T(8,128)(2,1)}, u32[]{:S(2)}) copy-start(bf16[512,256]{1,0:T(8,128)(2,1)} %wdown_ref.1) | copy-start | bytes 786436
  3.4 31.8 %copy-start.5 = (bf16[256,256]{1,0:T(8,128)(2,1)S(1)}, bf16[256,256]{1,0:T(8,128)(2,1)}, u32[]{:S(2)}) copy-start(bf16[256,256]{1,0:T(8,128)(2,1)} %wout_ref.1) | copy-start | bytes 393220
  3.4 31.8 %all-to-all-start = ((bf16[32,32,256]{2,1,0:T(8,128)(2,1)}), bf16[32,32,256]{2,1,0:T(8,128)(2,1)S(1)}, u32[]{:S(2)}, u32[]{:S(2)}) async-start(bf16[32,32,256]{2,1,0:T(8,128)(2,1)} %shard_map.118), calls=%async_computation | async-start | bytes 1048576 | tf_op jit(solution)/shard_map/all_to_all | solution.py:327
  17.9 17.3 %copy-start.6 = (f32[2,256]{1,0:T(2,128)S(1)}, f32[2,256]{1,0:T(2,128)}, u32[]{:S(2)}) copy-start(f32[2,256]{1,0:T(2,128)} %gains_ref.3) | copy-start | bytes 6148
  43.2 4.6 %collective-permute-start = (bf16[3072,128]{1,0:T(8,128)(2,1)S(1)}, bf16[3072,128]{1,0:T(8,128)(2,1)S(1)}, u32[]{:S(2)}, u32[]{:S(2)}) collective-permute-start(bf16[3072,128]{1,0:T(8,128)(2,1)S(1)} %get-tuple-element.33), channel_id=1, source_target_pairs={{0,1},{1,0},{2,3},{3,2},{4,5},{5,4},{6,7},{7,6},{8,9},{9,8},{10,11... | collective-permute-start | bytes 2359304 | tf_op jit(solution)/shard_map/ppermute | solution.py:348
  75.5 12.2 %collective-permute-start.1 = (bf16[16,64,128]{2,1,0:T(8,128)(2,1)S(1)}, bf16[16,64,128]{2,1,0:T(8,128)(2,1)S(1)}, u32[]{:S(2)}, u32[]{:S(2)}) collective-permute-start(bf16[16,64,128]{2,1,0:T(8,128)(2,1)S(1)} %get-tuple-element.36), channel_id=1, source_target_pairs={{0,32},{32,0},{1,33},{33,1},{2,34},{34,2},{3,35},{35,3},{4,36},{36... | collective-permute-start | bytes 786440 | tf_op jit(solution)/shard_map/ppermute | solution.py:361
  105.5 8.5 %collective-permute-start.2 = (bf16[3072,128]{1,0:T(8,128)(2,1)S(1)}, bf16[3072,128]{1,0:T(8,128)(2,1)S(1)}, u32[]{:S(2)}, u32[]{:S(2)}) collective-permute-start(bf16[3072,128]{1,0:T(8,128)(2,1)S(1)} %shard_map.124), channel_id=1, source_target_pairs={{0,1},{1,0},{2,3},{3,2},{4,5},{5,4},{6,7},{7,6},{8,9},{9,8},{10,11... | collective-permute-start | bytes 2359304 | tf_op jit(solution)/shard_map/ppermute | solution.py:371

commit v3 on v2

--- a/solution.py
+++ b/solution.py
@@ -14,6 +14,7 @@
 BF, F32 = jnp.bfloat16, jnp.float32
 LANES = 128
 AXES = ("y", "l", "x", "h", "c")
+SIDES = CORES = 2
 MIB = 1024 * 1024
 
 
@@ -42,13 +43,17 @@
     zlen = rows // pixels
     size = width // HEADS
     wide = HEADS * zlen
-    hidden_units = wup_ref.shape[1]
+    per = pixels // SIDES
+    sections = half // per
 
     at = lax.broadcasted_iota(jnp.int32, (rows, rows), 0)
     to = lax.broadcasted_iota(jnp.int32, (rows, rows), 1)
-    order = jnp.where(to == (at % zlen) * pixels + at // zlen, 1.0, 0.0).astype(BF)
-    x = dot(order, xg_ref[:, :half, :].reshape(rows, width))
-    g = dot(order, xg_ref[:, half:, :].reshape(rows, width))
+    pixel, section = at // zlen, at % zlen
+    device = ((section // (CORES * sections)) * SIDES + pixel // per) * CORES + section // sections % CORES
+    order = jnp.where(to == device * half + section % sections * per + pixel % per, 1.0, 0.0).astype(BF)
+    xg = xg_ref[...].astype(F32)
+    x = dot(order, xg[:, :half, :].reshape(rows, width).astype(BF))
+    g = dot(order, xg[:, half:, :].reshape(rows, width).astype(BF))
     g_low = g.astype(BF)
     g_ref[...] = g_low
     gain1, gain2 = gains_ref[0:1, :], gains_ref[1:2, :]
@@ -123,56 +128,87 @@
     ge = dot(dproj, wqkv_ref[...], (1, 1)) * gain1
     dxa = (r1 * ge - x * (r1 * r1 * r1) * jnp.mean(ge * x, -1, keepdims=True)).astype(BF)
     dx = (dh_low.astype(F32) + dxa.astype(F32)).astype(BF)
-    dx = dot(order, dx, (0, 0)).reshape(sources // 2, 2, half, width)
-    lanes(dx_ref, lanes(dx_ref, 0, dx[:, 0]), dx[:, 1])
-
-
-def weights_kernel(
-    place_ref, dx_ref, ub_ref, dproj_ref, mixed_ref, dh_ref, wb_ref, dpre_ref, mb_ref, g_ref, send_ref, keep_ref
-):
-    def fill(attention, mlp):
-        lanes(mlp, lanes(mlp, 0, dot(wb_ref[...], dpre_ref[...], (0, 0))), dot(mb_ref[...], g_ref[...], (0, 0)))
-        lanes(
-            attention,
-            lanes(attention, 0, dot(ub_ref[...], dproj_ref[...], (0, 0))),
-            dot(mixed_ref[...], dh_ref[...], (0, 0)),
-        )
-
-    pack = keep_ref.shape[0]
+    dx = dot(order, dx, (0, 0)).reshape(sources, half, width)
+    dx = jnp.concatenate([dx[..., i * LANES : (i + 1) * LANES] for i in range(width // LANES)], axis=1)
+    dx_ref[...] = dx.astype(BF).reshape(dx_ref.shape)
+
+
+def attention_half(out_ref, factors):
+    ub_ref, dproj_ref, mixed_ref, dh_ref = factors[:4]
+    start = lanes(out_ref, 0, dot(ub_ref[...], dproj_ref[...], (0, 0)))
+    lanes(out_ref, start, dot(mixed_ref[...], dh_ref[...], (0, 0)))
+
+
+def mlp_half(out_ref, factors):
+    wb_ref, dpre_ref, mb_ref, g_ref = factors[4:]
+    start = lanes(out_ref, 0, dot(wb_ref[...], dpre_ref[...], (0, 0)))
+    lanes(out_ref, start, dot(mb_ref[...], g_ref[...], (0, 0)))
+
+
+def send_kernel(place_ref, dx_ref, *refs):
+    *factors, send_ref = refs
     chips, tall = dx_ref.shape[:2]
+    pack = send_ref.shape[0] - chips * tall
 
     @pl.when(place_ref[0] == 0)
     def _():
-        fill(keep_ref, send_ref)
+        mlp_half(send_ref, factors)
 
     @pl.when(place_ref[0] != 0)
     def _():
-        fill(send_ref, keep_ref)
+        attention_half(send_ref, factors)
         for chip in range(chips):
             send_ref[pack + chip * tall : pack + (chip + 1) * tall, :] = dx_ref[chip]
 
 
-def arrange_kernel(x_ref, g_ref, out_ref):
+def keep_kernel(place_ref, *refs):
+    *factors, keep_ref = refs
+
+    @pl.when(place_ref[0] == 0)
+    def _():
+        attention_half(keep_ref, factors)
+
+    @pl.when(place_ref[0] != 0)
+    def _():
+        mlp_half(keep_ref, factors)
+
+
+def mixed_rows(first, second):
+    rows = first.shape[1]
+    upper = lax.broadcasted_iota(jnp.int32, first.shape, 1) < rows // 2
+    turned = [pltpu.roll(block, rows // 2, 1) for block in (first, second)]
+    return jnp.where(upper, first, turned[1]), jnp.where(upper, turned[0], second)
+
+
+def arrange_kernel(x_hbm, g_hbm, out_ref, x_ref, g_ref, done):
     peers, _, width = out_ref.shape
-    parts = [
-        ref[z].astype(F32).reshape(peers, -1, width) for ref in (x_ref, g_ref) for z in range(x_ref.shape[0])
-    ]
-    out_ref[...] = jnp.concatenate(parts, axis=1).astype(BF)
+    copies = []
+    for i, (source, target) in enumerate(((x_hbm, x_ref), (g_hbm, g_ref))):
+        for z in range(source.shape[0]):
+            copies.append(pltpu.make_async_copy(source.at[z], target.at[z], done.at[2 * i + z]))
+    for copy in copies:
+        copy.start()
+    for copy in copies:
+        copy.wait()
+    parts = [mixed_rows(*(ref[z].astype(F32).reshape(peers // 2, -1, width) for z in range(2))) for ref in (x_ref, g_ref)]
+    out_ref[...] = (
+        jnp.stack([jnp.concatenate(pair, axis=1) for pair in zip(*parts)], axis=1).reshape(out_ref.shape).astype(BF)
+    )
 
 
 def pair_kernel(place_ref, mine_ref, other_ref, dx_ref, out_ref):
     pack = mine_ref.shape[0]
-    chips, tall = dx_ref.shape[:2]
-    own = pack // out_ref.shape[0]
-    for to in range(out_ref.shape[0]):
+    count, tall = dx_ref.shape[:2]
+    own = pack // count
+    for to in range(count):
         rows = slice(to * own, (to + 1) * own)
         out_ref[to, :own, :] = (mine_ref[rows, :].astype(F32) + other_ref[rows, :].astype(F32)).astype(BF)
 
     @pl.when(place_ref[0] == 0)
     def _():
-        for chip in range(chips):
-            out_ref[2 * chip, own:, :] = dx_ref[chip]
-            out_ref[2 * chip + 1, own:, :] = other_ref[pack + chip * tall : pack + (chip + 1) * tall, :]
+        for to in range(count):
+            out_ref[to, own : own + tall, :] = dx_ref[to]
+            out_ref[to, own + tall :, :] = other_ref[pack + to * tall : pack + (to + 1) * tall, :]
 
 
 def total_of(ref, rows):
@@ -182,46 +218,27 @@
     return total.astype(BF)
 
 
-def first_sum_kernel(place_ref, in_ref, out_ref, stay_ref, pass_ref):
+def first_sum_kernel(place_ref, in_ref, out_ref, own_ref, next_ref):
     own = out_ref.shape[1]
     low = total_of(in_ref, own)
     for i in range(out_ref.shape[0]):
         out_ref[i] = low
 
-    def sort(side):
-        for chip in range(stay_ref.shape[0]):
-            stay_ref[chip] = in_ref[2 * chip + side, own:, :]
-            pass_ref[chip] = in_ref[2 * chip + 1 - side, own:, :]
-
-    @pl.when(place_ref[1] == 0)
-    def _():
-        sort(0)
-
-    @pl.when(place_ref[1] != 0)
-    def _():
-        sort(1)
-
-
-def second_sum_kernel(place_ref, in_ref, stay_ref, passed_ref, out_ref, own_ref, next_ref):
+    @pl.when(place_ref[0] == 0)
+    def _():
+        tall = own_ref.shape[0] // (CORES * in_ref.shape[0])
+        for piece in range(in_ref.shape[0]):
+            for core in range(CORES):
+                at = slice((CORES * piece + core) * tall, (CORES * piece + core + 1) * tall)
+                start = own + CORES * core * tall
+                own_ref[at, :] = in_ref[piece, start : start + tall, :]
+                next_ref[at, :] = in_ref[piece, start + tall : start + 2 * tall, :]
+
+
+def second_sum_kernel(in_ref, out_ref):
     low = total_of(in_ref, in_ref.shape[1])
     for i in range(out_ref.shape[0]):
         out_ref[i] = low
-    chips, tall = stay_ref.shape[0], stay_ref.shape[1] // 2
-
-    def sort(blocks):
-        for chip in range(chips):
-            for core in range(2):
-                at = slice((2 * chip + core) * tall, (2 * chip + core + 1) * tall)
-                own_ref[at, :] = blocks[core][chip, :tall, :]
-                next_ref[at, :] = blocks[core][chip, tall:, :]
-
-    @pl.when(place_ref[1] == 0)
-    def _():
-        sort((stay_ref, passed_ref))
-
-    @pl.when(place_ref[1] != 0)
-    def _():
-        sort((passed_ref, stay_ref))
 
 
 def join_kernel(mine_ref, next_ref, out_ref):
@@ -231,11 +248,12 @@
 
 
 def finish_kernel(
-    factor, near, place_ref, mine_ref, other_ref, own_ref, wqkv_ref, wup_ref, gains_ref,
+    factor, piece, place_ref, mine_ref, other_ref, own_ref, wqkv_ref, wup_ref, gains_ref,
     input_ref, qkv_ref, out_ref, up_ref, down_ref, ggains_ref,
 ):
     pack = mine_ref.shape[0]
     sections, pixels, width = input_ref.shape
+
     def columns(half, start, ref):
         tall = ref.shape[0]
         for i in range(ref.shape[1] // LANES):
@@ -249,13 +267,13 @@
         columns(mlp, columns(mlp, 0, up_ref), down_ref)
 
     def arrange(rows):
-        blocks = rows.astype(F32).reshape(pixels // near, -1, LANES)
-        for i in range(width // LANES):
-            for z in range(sections):
-                at = (i * sections + z) * near
-                input_ref[z, :, i * LANES : (i + 1) * LANES] = (
-                    blocks[:, at : at + near, :].reshape(pixels, LANES).astype(BF)
-                )
+        groups = width // LANES
+        blocks = rows.astype(F32).reshape(-1, CORES, piece, LANES)
+        tall = blocks.shape[2] // groups
+        for i in range(groups):
+            at = slice(i * tall, (i + 1) * tall)
+            for z, block in enumerate(mixed_rows(blocks[:, 0, at, :], blocks[:, 1, at, :])):
+                input_ref[z, :, i * LANES : (i + 1) * LANES] = block.reshape(pixels, LANES).astype(BF)
 
     @pl.when(place_ref[0] == 0)
     def _():
@@ -272,8 +290,8 @@
     ggains_ref[...] = jnp.stack([one, two]) / gains_ref[...]
 
 
-def call(kernel, outs, args, scratch=(), placed=False, room=6):
-    specs = [pl.BlockSpec(memory_space=pltpu.VMEM)] * len(args)
+def call(kernel, outs, args, scratch=(), placed=False, room=6, spaces=None):
+    specs = [pl.BlockSpec(memory_space=space) for space in spaces or [pltpu.VMEM] * len(args)]
     if placed:
         specs[0] = pl.BlockSpec(memory_space=pltpu.SMEM)
     single = not isinstance(outs, (list, tuple))
@@ -314,17 +332,25 @@
 
 def body(features, grad_output, qkv_weight, out_weight, up_weight, down_weight, norm_gains):
     sections, pixels, width = features.shape
-    peers = lax.axis_size(("x", "h", "c"))
-    near = pixels // peers
+    around = ("x", "h", "l", "c")
+    peers = lax.axis_size(around)
+    near = SIDES * pixels // peers
     hidden = up_weight.shape[1]
     place = jnp.stack([lax.axis_index("c"), lax.axis_index("l")]).astype(jnp.int32)
-    rows = peers * sections * near
-    zlen = peers * sections
+    zlen = sections * peers // SIDES
+    rows = near * zlen
     pack = (width * 4 * width) // LANES
-    chips = peers // 2
-    tall = 2 * sections * near * width // LANES
-    both = call(arrange_kernel, shape((peers, 2 * sections * near, width)), (features, grad_output))
-    xg = lax.all_to_all(both, ("x", "h", "c"), split_axis=0, concat_axis=0, tiled=True)
+    chips = peers // CORES
+    tall = rows * width // LANES // chips
+    both = call(
+        arrange_kernel,
+        shape((peers, sections * near, width)),
+        (features, grad_output),
+        scratch=[pltpu.VMEM(features.shape, BF)] * 2 + [pltpu.SemaphoreType.DMA((2 * sections,))],
+        spaces=[pl.ANY, pl.ANY],
+        room=60,
+    )
+    xg = lax.all_to_all(both, around, split_axis=0, concat_axis=0, tiled=True)
     wide = [3 * width, width, width, width, hidden, hidden, width]
     dx, *factors = call(
         functools.partial(block_kernel, near),
@@ -337,41 +363,32 @@
         ],
         room=16,
     )
-    send, keep = call(
-        weights_kernel,
-        [shape((pack + chips * tall, LANES)), shape((pack, LANES))],
-        (place, dx, *factors),
-        placed=True,
-        room=12,
+    send = call(
+        send_kernel, shape((pack + chips * tall, LANES)), (place, dx, *factors), placed=True, room=12
     )
     swap = [(0, 1), (1, 0)]
     other = lax.ppermute(send, "c", swap)
+    keep = call(keep_kernel, shape((pack, LANES)), (place, *factors), placed=True, room=12)
     wide_groups = groups_of((("x", "h", "l"), ("x", "y")))
     line_groups = groups_of((("y",), ("l", "h")))
     slab, line = len(wide_groups[0]), len(line_groups[0])
     own = pack // slab
-    pieces = call(pair_kernel, shape((slab, own + tall, LANES)), (place, keep, other, dx), placed=True)
+    pieces = call(pair_kernel, shape((slab, own + CORES * tall, LANES)), (place, keep, other, dx), placed=True)
     pieces = exchange(pieces, wide_groups)
-    copies, stay, onward = call(
+    copies, own_rows, next_rows = call(
         first_sum_kernel,
-        [shape((line, own, LANES))] + [shape((chips, tall, LANES))] * 2,
+        [shape((line, own, LANES))] + [shape((chips * tall, LANES))] * 2,
         (place, pieces),
         placed=True,
     )
-    passed = lax.ppermute(onward, "l", swap)
     pieces = exchange(copies, line_groups)
-    copies, own_rows, next_rows = call(
-        second_sum_kernel,
-        [shape((slab, own, LANES))] + [shape((chips * tall, LANES))] * 2,
-        (place, pieces, stay, passed),
-        placed=True,
-    )
+    copies = call(second_sum_kernel, shape((slab, own, LANES)), (pieces,))
     mine = exchange(copies, wide_groups).reshape(pack, LANES)
     joined = call(join_kernel, shape((pack + chips * tall, LANES)), (mine, next_rows))
     other = lax.ppermute(joined, "c", swap)
-    voxels = sections * peers * pixels * lax.axis_size(("y", "l"))
+    voxels = zlen * pixels * lax.axis_size(("y", "l"))
     return tuple(call(
-        functools.partial(finish_kernel, float(voxels) ** (-0.5), near),
+        functools.partial(finish_kernel, float(voxels) ** (-0.5), tall // CORES),
         [
             shape(features.shape),
             shape((width, 3 * width), F32),

time: 117 us -> 113 us (0.966)
  starting transfers between devices: 26.8 us -> 24.3 us
  local copies, waits for them, and re-layouts: 1.91 us -> 0.03 us
  Pallas kernels: 13 us -> 14.5 us
    ppermute x1 -> x0, starting transfers between devices: 2.9 us -> none  [body(): passed = lax.ppermute(onward, 'l', swap)]
    unnamed x14 -> x10, local copies, waits for them, and re-layouts: 1.91 us -> 0.03 us
    pallas_call x8 -> x9, Pallas kernels: 13 us -> 14.5 us  [call(): pl.pallas_call(kernel, out_shape=outs, in_specs=specs, out_specs=pl.Block...]
  transfers between devices with their start and end apart: 4 -> 3, of which waited for: 3 -> 3; matrix products, arithmetic and copies ran while one was open for 0% -> 0% of each run, Pallas kernels for 0% -> 1%
where the time goes in v3:
time: 113 us
  blocking collectives  53.1 us (47%)
  starting transfers between devices  24.3 us (22%)
  waiting for transfers between devices  20 us (18%)
  Pallas kernels  14.5 us (13%)
    all_to_all x3, blocking collectives, exchange(): lax.all_to_all(pieces, AXES, split_axis=0, concat_axis=0, axis_index_grou...  53.1 us
    all_to_all x1, waiting for transfers between devices, body(): xg = lax.all_to_all(both, around, split_axis=0, concat_axis=0, tiled=True)  17.2 us
    all_to_all x1, starting transfers between devices, body(): xg = lax.all_to_all(both, around, split_axis=0, concat_axis=0, tiled=True)  15 us
    pallas_call x9, Pallas kernels, call(): pl.pallas_call(kernel, out_shape=outs, in_specs=specs, out_specs=pl.Block...  14.5 us
    ppermute x1, starting transfers between devices, body(): other = lax.ppermute(joined, 'c', swap)  7.12 us
  transfers between devices with their start and end apart: 3, of which 3 were waited for; matrix products, arithmetic and copies ran while one was open for 0% of the time, Pallas kernels for 1%

profile of v3, /device:TPU:1, one launch (start us, length us, event | category | flops | bytes accessed | tf_op | source)
XLA Modules:
  0.0 112.8 jit_solution(10108393276567476533)
XLA Ops:
  0.6 2.0 %shard_map.118 = bf16[64,16,256]{2,1,0:T(8,128)(2,1)} custom-call(bf16[2,256,256]{2,1,0:T(8,128)(2,1)} %x_hbm.1, bf16[2,256,256]{2,1,0:T(8,128)(2,1)} %g_hbm.1), custom_call_target="tpu_custom_call" | custom-call | tf_op jit(solution)/shard_map/pallas_call | solution.py:298
  2.7 0.0 copy-start
  2.7 0.0 copy-start.1
  2.7 0.0 copy-start.2
  2.7 0.0 copy-start.3
  2.7 15.0 %all-to-all-start = ((bf16[64,16,256]{2,1,0:T(8,128)(2,1)}), bf16[64,16,256]{2,1,0:T(8,128)(2,1)S(1)}, u32[]{:S(2)}, u32[]{:S(2)}) async-start(bf16[64,16,256]{2,1,0:T(8,128)(2,1)} %shard_map.118), calls=%async_computation | async-start | bytes 1048576 | tf_op jit(solution)/shard_map/all_to_all | solution.py:353
  17.7 0.0 copy-start.4
  17.7 0.1 pad_add_fusion.place_ref
  17.8 17.2 %all-to-all-done.xg_ref = bf16[64,16,256]{2,1,0:T(8,128)(2,1)S(1)} async-done(((bf16[64,16,256]{2,1,0:T(8,128)(2,1)}), bf16[64,16,256]{2,1,0:T(8,128)(2,1)S(1)}, u32[]{:S(2)}, u32[]{:S(2)}) %all-to-all-start) | async-done | bytes 524320 | tf_op jit(solution)/shard_map/all_to_all | solution.py:353
  35.1 6.9 %shard_map.119 = (bf16[32,32,128]{2,1,0:T(8,128)(2,1)S(1)}, bf16[512,256]{1,0:T(8,128)(2,1)S(1)}, bf16[512,768]{1,0:T(8,128)(2,1)S(1)}, bf16[512,256]{1,0:T(8,12...) custom-call(bf16[64,16,256]{2,1,0:T(8,128)(2,1)S(1)} %all-to-all-don, ...), custom_call_target="tpu_custom_call" | custom-call | tf_op jit(solution)/shard_map/pallas_call | solution.py:298
  41.9 1.0 shard_map.121
  43.0 2.2 %collective-permute-start = (bf16[3072,128]{1,0:T(8,128)(2,1)S(1)}, bf16[3072,128]{1,0:T(8,128)(2,1)S(1)}, u32[]{:S(2)}, u32[]{:S(2)}) collective-permute-start(bf16[3072,128]{1,0:T(8,128)(2,1)S(1)} %shard_map.121), channel_id=1, source_target_pairs={{0,1},{1,0},{2,3},{3,2},{4,5},{5,4},{6,7},{7,6},{8,9},{9,8},{10,11... | collective-permute-start | bytes 2359304 | tf_op jit(solution)/shard_map/ppermute | solution.py:370
  45.2 1.0 shard_map.120.mine_ref
  46.2 0.9 collective-permute-done.other_ref
  47.1 0.7 shard_map.122
  47.8 26.1 %all_to_all.20.in_ref = bf16[32,128,128]{2,1,0:T(8,128)(2,1)S(1)} all-to-all(bf16[32,128,128]{2,1,0:T(8,128)(2,1)S(1)} %shard_map.122), channel_id=1, replica_groups={{0,32,2,34,4,36,6,38,8,40,10,42,12,44,14,46,16,48,18,50,20,52,22,54,24,..., dimensions={0} | all-to-all | bytes 2097152 | tf_op jit(solution)/shard_map/all_to_all | solution.py:328
  73.9 0.6 shard_map.123
  74.5 9.7 %all_to_all.21.in_ref = bf16[8,64,128]{2,1,0:T(8,128)(2,1)S(1)} all-to-all(bf16[8,64,128]{2,1,0:T(8,128)(2,1)S(1)} %get-tuple-element.27), channel_id=1, replica_groups={{0,64,128,192,256,320,384,448},{2,66,130,194,258,322,386,450},{4,68,132..., dimensions={0} | all-to-all | bytes 262144 | tf_op jit(solution)/shard_map/all_to_all | solution.py:328
  84.3 0.1 shard_map.124
  84.3 17.2 %all_to_all.22 = bf16[32,64,128]{2,1,0:T(8,128)(2,1)S(1)} all-to-all(bf16[32,64,128]{2,1,0:T(8,128)(2,1)S(1)} %shard_map.124), channel_id=1, replica_groups={{0,32,2,34,4,36,6,38,8,40,10,42,12,44,14,46,16,48,18,50,20,52,22,54,24,..., dimensions={0} | all-to-all | bytes 1048576 | tf_op jit(solution)/shard_map/all_to_all | solution.py:328
  101.6 0.1 shard_map.125
  101.6 7.1 %collective-permute-start.1 = (bf16[3072,128]{1,0:T(8,128)(2,1)S(1)}, bf16[3072,128]{1,0:T(8,128)(2,1)S(1)}, u32[]{:S(2)}, u32[]{:S(2)}) collective-permute-start(bf16[3072,128]{1,0:T(8,128)(2,1)S(1)} %shard_map.125), channel_id=1, source_target_pairs={{0,1},{1,0},{2,3},{3,2},{4,5},{5,4},{6,7},{7,6},{8,9},{9,8},{10,11... | collective-permute-start | bytes 2359304 | tf_op jit(solution)/shard_map/ppermute | solution.py:388
  108.8 1.9 %collective-permute-done.1.other_ref = bf16[3072,128]{1,0:T(8,128)(2,1)S(1)} collective-permute-done((bf16[3072,128]{1,0:T(8,128)(2,1)S(1)}, bf16[3072,128]{1,0:T(8,128)(2,1)S(1)}, u32[]{:S(2)}, u32[]{:S(2)}) %collective-permute-start.1) | collective-permute-done | bytes 786464 | tf_op jit(solution)/shard_map/ppermute | solution.py:388
  110.6 2.2 %shard_map.126 = (bf16[2,256,256]{2,1,0:T(8,128)(2,1)}, f32[256,768]{1,0:T(8,128)}, f32[256,256]{1,0:T(8,128)}, f32[256,512]{1,0:T(8,128)}, f32[512,256]{1,0:T(8,128)}, /*index=5*/f32[2,256]{1,0:T(2,128)}) custom-call(s32[2]{0:T(128)S(1)} %pad_add_fusion.place_ref, bf16[2048,128]{1,0:T(8,128)(2,1)S(1)} %bitcast.4, ...), custom_call_target="tpu_custom_call" | custom-call | tf_op jit(solution)/shard_map/pallas_call | solution.py:298
  (5 shorter events, 0.0 us)
Async XLA Ops:
  2.7 32.4 %copy-start = (bf16[256,768]{1,0:T(8,128)(2,1)S(1)}, bf16[256,768]{1,0:T(8,128)(2,1)}, u32[]{:S(2)}) copy-start(bf16[256,768]{1,0:T(8,128)(2,1)} %wqkv_ref.3) | copy-start | bytes 1179652
  2.7 32.4 %copy-start.1 = (bf16[256,512]{1,0:T(8,128)(2,1)S(1)}, bf16[256,512]{1,0:T(8,128)(2,1)}, u32[]{:S(2)}) copy-start(bf16[256,512]{1,0:T(8,128)(2,1)} %wup_ref.3) | copy-start | bytes 786436
  2.7 32.3 %copy-start.2 = (bf16[512,256]{1,0:T(8,128)(2,1)S(1)}, bf16[512,256]{1,0:T(8,128)(2,1)}, u32[]{:S(2)}) copy-start(bf16[512,256]{1,0:T(8,128)(2,1)} %wdown_ref.1) | copy-start | bytes 786436
  2.7 32.3 %copy-start.3 = (bf16[256,256]{1,0:T(8,128)(2,1)S(1)}, bf16[256,256]{1,0:T(8,128)(2,1)}, u32[]{:S(2)}) copy-start(bf16[256,256]{1,0:T(8,128)(2,1)} %wout_ref.1) | copy-start | bytes 393220
  2.7 32.3 %all-to-all-start = ((bf16[64,16,256]{2,1,0:T(8,128)(2,1)}), bf16[64,16,256]{2,1,0:T(8,128)(2,1)S(1)}, u32[]{:S(2)}, u32[]{:S(2)}) async-start(bf16[64,16,256]{2,1,0:T(8,128)(2,1)} %shard_map.118), calls=%async_computation | async-start | bytes 1048576 | tf_op jit(solution)/shard_map/all_to_all | solution.py:353
  17.7 17.3 %copy-start.4 = (f32[2,256]{1,0:T(2,128)S(1)}, f32[2,256]{1,0:T(2,128)}, u32[]{:S(2)}) copy-start(f32[2,256]{1,0:T(2,128)} %gains_ref.3) | copy-start | bytes 6148
  43.0 4.2 %collective-permute-start = (bf16[3072,128]{1,0:T(8,128)(2,1)S(1)}, bf16[3072,128]{1,0:T(8,128)(2,1)S(1)}, u32[]{:S(2)}, u32[]{:S(2)}) collective-permute-start(bf16[3072,128]{1,0:T(8,128)(2,1)S(1)} %shard_map.121), channel_id=1, source_target_pairs={{0,1},{1,0},{2,3},{3,2},{4,5},{5,4},{6,7},{7,6},{8,9},{9,8},{10,11... | collective-permute-start | bytes 2359304 | tf_op jit(solution)/shard_map/ppermute | solution.py:370
  101.6 9.0 %collective-permute-start.1 = (bf16[3072,128]{1,0:T(8,128)(2,1)S(1)}, bf16[3072,128]{1,0:T(8,128)(2,1)S(1)}, u32[]{:S(2)}, u32[]{:S(2)}) collective-permute-start(bf16[3072,128]{1,0:T(8,128)(2,1)S(1)} %shard_map.125), channel_id=1, source_target_pairs={{0,1},{1,0},{2,3},{3,2},{4,5},{5,4},{6,7},{7,6},{8,9},{9,8},{10,11... | collective-permute-start | bytes 2359304 | tf_op jit(solution)/shard_map/ppermute | solution.py:388

commit v4 on v3

--- a/solution.py
+++ b/solution.py
@@ -84,12 +84,15 @@
 
     for pixel in range(pixels):
         query, keys, values = (rows_of(proj_ref, pixel, i) for i in range(3))
-        scores = dot(keys, spread(query), (1, 1)) * scale
+        probs_ref[pixel] = dot(keys, spread(query), (1, 1)) * scale
+    for pixel in range(pixels):
+        scores = probs_ref[pixel]
         raised = jnp.exp(scores - jnp.max(scores, 0, keepdims=True))
         probs = raised * (1.0 / jnp.sum(raised, 0, keepdims=True))
         probs_ref[pixel] = probs
+    for pixel in range(pixels):
         mixed_ref[pixel * zlen : (pixel + 1) * zlen, :] = gathered(
-            dot(probs.astype(BF), values, (0, 0))
+            dot(probs_ref[pixel].astype(BF), rows_of(proj_ref, pixel, 2), (0, 0))
         ).astype(BF)
 
     mixed = mixed_ref[...]
@@ -97,32 +100,33 @@
     r2 = lax.rsqrt(jnp.mean(h * h, -1, keepdims=True) + EPS)
     wb = (h * r2 * gain2).astype(BF)
     wb_ref[...] = wb
-    pre = dot(wb, wup_ref[...])
-    act = jax.nn.sigmoid(pre)
-    mb_ref[...] = (pre * act).astype(BF)
-    dmb = dot(g_low, wdown_ref[...], (1, 1))
-    dpre = (dmb * act * (1.0 + pre * (1.0 - act))).astype(BF)
-    dpre_ref[...] = dpre
-    gd = dot(dpre, wup_ref[...], (1, 1)) * gain2
+    cuts = [slice(i * rows // 2, (i + 1) * rows // 2) for i in range(2)]
+    pres = [dot(wb[cut], wup_ref[...]) for cut in cuts]
+    dmbs = [dot(g_low[cut], wdown_ref[...], (1, 1)) for cut in cuts]
+    dws = []
+    for cut, pre, dmb in zip(cuts, pres, dmbs):
+        act = jax.nn.sigmoid(pre)
+        mb_ref[cut, :] = (pre * act).astype(BF)
+        dpre = (dmb * act * (1.0 + pre * (1.0 - act))).astype(BF)
+        dpre_ref[cut, :] = dpre
+        dws.append(dot(dpre, wup_ref[...], (1, 1)))
+    gd = jnp.concatenate(dws, axis=0) * gain2
     dh_low = (g + (r2 * gd - h * (r2 * r2 * r2) * jnp.mean(gd * h, -1, keepdims=True))).astype(BF)
     dh_ref[...] = dh_low
     dmixed_ref[...] = dot(dh_low, wout_ref[...], (1, 1)).astype(BF)
 
+    dprobs = [dot(rows_of(proj_ref, pixel, 2), spread(rows_of(dmixed_ref, pixel, 0)), (1, 1)) for pixel in range(pixels)]
+    dvalues = [dot(probs_ref[pixel].astype(BF), spread(rows_of(dmixed_ref, pixel, 0))) for pixel in range(pixels)]
+    dscores = []
+    for pixel in range(pixels):
+        probs = probs_ref[pixel]
+        dscores.append((probs * (dprobs[pixel] - jnp.sum(probs * dprobs[pixel], 0, keepdims=True)) * scale).astype(BF))
     for pixel in range(pixels):
         query, keys, values = (rows_of(proj_ref, pixel, i) for i in range(3))
-        spread_grad = spread(rows_of(dmixed_ref, pixel, 0))
-        probs = probs_ref[pixel]
-        dprobs = dot(values, spread_grad, (1, 1))
-        dvalues = dot(probs.astype(BF), spread_grad)
-        dscores = (
-            probs * (dprobs - jnp.sum(probs * dprobs, 0, keepdims=True)) * scale
-        ).astype(BF)
-        dkeys = dot(dscores, spread(query))
-        dquery = gathered(dot(dscores, keys, (0, 0)))
         here = slice(pixel * zlen, (pixel + 1) * zlen)
-        dproj_ref[here, :width] = dquery.astype(BF)
-        dproj_ref[here, width : 2 * width] = dkeys.astype(BF)
-        dproj_ref[here, 2 * width :] = dvalues.astype(BF)
+        dproj_ref[here, :width] = gathered(dot(dscores[pixel], keys, (0, 0))).astype(BF)
+        dproj_ref[here, width : 2 * width] = dot(dscores[pixel], spread(query)).astype(BF)
+        dproj_ref[here, 2 * width :] = dvalues[pixel].astype(BF)
 
     dproj = dproj_ref[...]
     ge = dot(dproj, wqkv_ref[...], (1, 1)) * gain1

time: 113 us -> 112 us (level)
  no operation moved by 1% of the time
where the time goes in v4:
time: 112 us
  blocking collectives  53.1 us (47%)
  starting transfers between devices  24.3 us (22%)
  waiting for transfers between devices  20 us (18%)
  Pallas kernels  13.4 us (12%)
    all_to_all x3, blocking collectives, exchange(): lax.all_to_all(pieces, AXES, split_axis=0, concat_axis=0, axis_index_grou...  53.1 us
    all_to_all x1, waiting for transfers between devices, body(): xg = lax.all_to_all(both, around, split_axis=0, concat_axis=0, tiled=True)  17.2 us
    all_to_all x1, starting transfers between devices, body(): xg = lax.all_to_all(both, around, split_axis=0, concat_axis=0, tiled=True)  15 us
    pallas_call x9, Pallas kernels, call(): pl.pallas_call(kernel, out_shape=outs, in_specs=specs, out_specs=pl.Block...  13.4 us
    ppermute x1, starting transfers between devices, body(): other = lax.ppermute(joined, 'c', swap)  7.11 us
  transfers between devices with their start and end apart: 3, of which 3 were waited for; matrix products, arithmetic and copies ran while one was open for 0% of the time, Pallas kernels for 1%

profile of v4, /device:TPU:1, one launch (start us, length us, event | category | flops | bytes accessed | tf_op | source)
XLA Modules:
  0.0 111.7 jit_solution(17212370193959905621)
XLA Ops:
  0.6 2.0 %shard_map.118 = bf16[64,16,256]{2,1,0:T(8,128)(2,1)} custom-call(bf16[2,256,256]{2,1,0:T(8,128)(2,1)} %x_hbm.1, bf16[2,256,256]{2,1,0:T(8,128)(2,1)} %g_hbm.1), custom_call_target="tpu_custom_call" | custom-call | tf_op jit(solution)/shard_map/pallas_call | solution.py:302
  2.7 0.0 copy-start
  2.7 0.0 copy-start.1
  2.7 0.0 copy-start.2
  2.7 0.0 copy-start.3
  2.7 15.0 %all-to-all-start = ((bf16[64,16,256]{2,1,0:T(8,128)(2,1)}), bf16[64,16,256]{2,1,0:T(8,128)(2,1)S(1)}, u32[]{:S(2)}, u32[]{:S(2)}) async-start(bf16[64,16,256]{2,1,0:T(8,128)(2,1)} %shard_map.118), calls=%async_computation | async-start | bytes 1048576 | tf_op jit(solution)/shard_map/all_to_all | solution.py:357
  17.7 0.0 copy-start.4
  17.7 0.1 pad_add_fusion.place_ref
  17.8 17.2 %all-to-all-done.xg_ref = bf16[64,16,256]{2,1,0:T(8,128)(2,1)S(1)} async-done(((bf16[64,16,256]{2,1,0:T(8,128)(2,1)}), bf16[64,16,256]{2,1,0:T(8,128)(2,1)S(1)}, u32[]{:S(2)}, u32[]{:S(2)}) %all-to-all-start) | async-done | bytes 524320 | tf_op jit(solution)/shard_map/all_to_all | solution.py:357
  35.1 5.7 %shard_map.119 = (bf16[32,32,128]{2,1,0:T(8,128)(2,1)S(1)}, bf16[512,256]{1,0:T(8,128)(2,1)S(1)}, bf16[512,768]{1,0:T(8,128)(2,1)S(1)}, bf16[512,256]{1,0:T(8,12...) custom-call(bf16[64,16,256]{2,1,0:T(8,128)(2,1)S(1)} %all-to-all-don, ...), custom_call_target="tpu_custom_call" | custom-call | tf_op jit(solution)/shard_map/pallas_call | solution.py:302
  40.8 1.0 shard_map.121
  41.9 2.2 %collective-permute-start = (bf16[3072,128]{1,0:T(8,128)(2,1)S(1)}, bf16[3072,128]{1,0:T(8,128)(2,1)S(1)}, u32[]{:S(2)}, u32[]{:S(2)}) collective-permute-start(bf16[3072,128]{1,0:T(8,128)(2,1)S(1)} %shard_map.121), channel_id=1, source_target_pairs={{0,1},{1,0},{2,3},{3,2},{4,5},{5,4},{6,7},{7,6},{8,9},{9,8},{10,11... | collective-permute-start | bytes 2359304 | tf_op jit(solution)/shard_map/ppermute | solution.py:374
  44.1 1.0 shard_map.120.mine_ref
  45.1 0.9 collective-permute-done.other_ref
  46.0 0.7 shard_map.122
  46.7 26.1 %all_to_all.20.in_ref = bf16[32,128,128]{2,1,0:T(8,128)(2,1)S(1)} all-to-all(bf16[32,128,128]{2,1,0:T(8,128)(2,1)S(1)} %shard_map.122), channel_id=1, replica_groups={{0,32,2,34,4,36,6,38,8,40,10,42,12,44,14,46,16,48,18,50,20,52,22,54,24,..., dimensions={0} | all-to-all | bytes 2097152 | tf_op jit(solution)/shard_map/all_to_all | solution.py:332
  72.8 0.6 shard_map.123
  73.4 9.7 %all_to_all.21.in_ref = bf16[8,64,128]{2,1,0:T(8,128)(2,1)S(1)} all-to-all(bf16[8,64,128]{2,1,0:T(8,128)(2,1)S(1)} %get-tuple-element.27), channel_id=1, replica_groups={{0,64,128,192,256,320,384,448},{2,66,130,194,258,322,386,450},{4,68,132..., dimensions={0} | all-to-all | bytes 262144 | tf_op jit(solution)/shard_map/all_to_all | solution.py:332
  83.2 0.1 shard_map.124
  83.2 17.3 %all_to_all.22 = bf16[32,64,128]{2,1,0:T(8,128)(2,1)S(1)} all-to-all(bf16[32,64,128]{2,1,0:T(8,128)(2,1)S(1)} %shard_map.124), channel_id=1, replica_groups={{0,32,2,34,4,36,6,38,8,40,10,42,12,44,14,46,16,48,18,50,20,52,22,54,24,..., dimensions={0} | all-to-all | bytes 1048576 | tf_op jit(solution)/shard_map/all_to_all | solution.py:332
  100.5 0.1 shard_map.125
  100.5 7.1 %collective-permute-start.1 = (bf16[3072,128]{1,0:T(8,128)(2,1)S(1)}, bf16[3072,128]{1,0:T(8,128)(2,1)S(1)}, u32[]{:S(2)}, u32[]{:S(2)}) collective-permute-start(bf16[3072,128]{1,0:T(8,128)(2,1)S(1)} %shard_map.125), channel_id=1, source_target_pairs={{0,1},{1,0},{2,3},{3,2},{4,5},{5,4},{6,7},{7,6},{8,9},{9,8},{10,11... | collective-permute-start | bytes 2359304 | tf_op jit(solution)/shard_map/ppermute | solution.py:392
  107.6 1.9 %collective-permute-done.1.other_ref = bf16[3072,128]{1,0:T(8,128)(2,1)S(1)} collective-permute-done((bf16[3072,128]{1,0:T(8,128)(2,1)S(1)}, bf16[3072,128]{1,0:T(8,128)(2,1)S(1)}, u32[]{:S(2)}, u32[]{:S(2)}) %collective-permute-start.1) | collective-permute-done | bytes 786464 | tf_op jit(solution)/shard_map/ppermute | solution.py:392
  109.5 2.2 %shard_map.126 = (bf16[2,256,256]{2,1,0:T(8,128)(2,1)}, f32[256,768]{1,0:T(8,128)}, f32[256,256]{1,0:T(8,128)}, f32[256,512]{1,0:T(8,128)}, f32[512,256]{1,0:T(8,128)}, /*index=5*/f32[2,256]{1,0:T(2,128)}) custom-call(s32[2]{0:T(128)S(1)} %pad_add_fusion.place_ref, bf16[2048,128]{1,0:T(8,128)(2,1)S(1)} %bitcast.4, ...), custom_call_target="tpu_custom_call" | custom-call | tf_op jit(solution)/shard_map/pallas_call | solution.py:302
  (5 shorter events, 0.0 us)
Async XLA Ops:
  2.7 32.4 %copy-start = (bf16[256,768]{1,0:T(8,128)(2,1)S(1)}, bf16[256,768]{1,0:T(8,128)(2,1)}, u32[]{:S(2)}) copy-start(bf16[256,768]{1,0:T(8,128)(2,1)} %wqkv_ref.3) | copy-start | bytes 1179652
  2.7 32.4 %copy-start.1 = (bf16[256,512]{1,0:T(8,128)(2,1)S(1)}, bf16[256,512]{1,0:T(8,128)(2,1)}, u32[]{:S(2)}) copy-start(bf16[256,512]{1,0:T(8,128)(2,1)} %wup_ref.3) | copy-start | bytes 786436
  2.7 32.3 %copy-start.2 = (bf16[512,256]{1,0:T(8,128)(2,1)S(1)}, bf16[512,256]{1,0:T(8,128)(2,1)}, u32[]{:S(2)}) copy-start(bf16[512,256]{1,0:T(8,128)(2,1)} %wdown_ref.1) | copy-start | bytes 786436
  2.7 32.3 %copy-start.3 = (bf16[256,256]{1,0:T(8,128)(2,1)S(1)}, bf16[256,256]{1,0:T(8,128)(2,1)}, u32[]{:S(2)}) copy-start(bf16[256,256]{1,0:T(8,128)(2,1)} %wout_ref.1) | copy-start | bytes 393220
  2.7 32.3 %all-to-all-start = ((bf16[64,16,256]{2,1,0:T(8,128)(2,1)}), bf16[64,16,256]{2,1,0:T(8,128)(2,1)S(1)}, u32[]{:S(2)}, u32[]{:S(2)}) async-start(bf16[64,16,256]{2,1,0:T(8,128)(2,1)} %shard_map.118), calls=%async_computation | async-start | bytes 1048576 | tf_op jit(solution)/shard_map/all_to_all | solution.py:357
  17.7 17.3 %copy-start.4 = (f32[2,256]{1,0:T(2,128)S(1)}, f32[2,256]{1,0:T(2,128)}, u32[]{:S(2)}) copy-start(f32[2,256]{1,0:T(2,128)} %gains_ref.3) | copy-start | bytes 6148
  41.9 4.2 %collective-permute-start = (bf16[3072,128]{1,0:T(8,128)(2,1)S(1)}, bf16[3072,128]{1,0:T(8,128)(2,1)S(1)}, u32[]{:S(2)}, u32[]{:S(2)}) collective-permute-start(bf16[3072,128]{1,0:T(8,128)(2,1)S(1)} %shard_map.121), channel_id=1, source_target_pairs={{0,1},{1,0},{2,3},{3,2},{4,5},{5,4},{6,7},{7,6},{8,9},{9,8},{10,11... | collective-permute-start | bytes 2359304 | tf_op jit(solution)/shard_map/ppermute | solution.py:374
  100.5 9.0 %collective-permute-start.1 = (bf16[3072,128]{1,0:T(8,128)(2,1)S(1)}, bf16[3072,128]{1,0:T(8,128)(2,1)S(1)}, u32[]{:S(2)}, u32[]{:S(2)}) collective-permute-start(bf16[3072,128]{1,0:T(8,128)(2,1)S(1)} %shard_map.125), channel_id=1, source_target_pairs={{0,1},{1,0},{2,3},{3,2},{4,5},{5,4},{6,7},{7,6},{8,9},{9,8},{10,11... | collective-permute-start | bytes 2359304 | tf_op jit(solution)/shard_map/ppermute | solution.py:392

commit v5 on v4

--- a/solution.py
+++ b/solution.py
@@ -15,6 +15,7 @@
 LANES = 128
 AXES = ("y", "l", "x", "h", "c")
 SIDES = CORES = 2
+LEAD = 1
 MIB = 1024 * 1024
 
 
@@ -137,32 +138,31 @@
     dx_ref[...] = dx.astype(BF).reshape(dx_ref.shape)
 
 
-def attention_half(out_ref, factors):
-    ub_ref, dproj_ref, mixed_ref, dh_ref = factors[:4]
-    start = lanes(out_ref, 0, dot(ub_ref[...], dproj_ref[...], (0, 0)))
+def first_part(out_ref, factors):
+    ub_ref, dproj_ref = factors[:2]
+    lanes(out_ref, 0, dot(ub_ref[...], dproj_ref[...], (0, 0)))
+
+
+def second_part(out_ref, factors):
+    mixed_ref, dh_ref, wb_ref, dpre_ref, mb_ref, g_ref = factors[2:]
+    start = lanes(out_ref, 0, dot(wb_ref[...], dpre_ref[...], (0, 0)))
+    start = lanes(out_ref, start, dot(mb_ref[...], g_ref[...], (0, 0)))
     lanes(out_ref, start, dot(mixed_ref[...], dh_ref[...], (0, 0)))
 
 
-def mlp_half(out_ref, factors):
-    wb_ref, dpre_ref, mb_ref, g_ref = factors[4:]
-    start = lanes(out_ref, 0, dot(wb_ref[...], dpre_ref[...], (0, 0)))
-    lanes(out_ref, start, dot(mb_ref[...], g_ref[...], (0, 0)))
-
-
-def send_kernel(place_ref, dx_ref, *refs):
+def send_kernel(pack, place_ref, dx_ref, *refs):
     *factors, send_ref = refs
-    chips, tall = dx_ref.shape[:2]
-    pack = send_ref.shape[0] - chips * tall
-
-    @pl.when(place_ref[0] == 0)
-    def _():
-        mlp_half(send_ref, factors)
-
-    @pl.when(place_ref[0] != 0)
-    def _():
-        attention_half(send_ref, factors)
-        for chip in range(chips):
-            send_ref[pack + chip * tall : pack + (chip + 1) * tall, :] = dx_ref[chip]
+    count, tall = dx_ref.shape[:2]
+
+    @pl.when(place_ref[0] == 0)
+    def _():
+        second_part(send_ref, factors)
+
+    @pl.when(place_ref[0] != 0)
+    def _():
+        first_part(send_ref, factors)
+        for to in range(count):
+            send_ref[pack + to * tall : pack + (to + 1) * tall, :] = dx_ref[to]
 
 
 def keep_kernel(place_ref, *refs):
@@ -170,11 +170,11 @@
 
     @pl.when(place_ref[0] == 0)
     def _():
-        attention_half(keep_ref, factors)
-
-    @pl.when(place_ref[0] != 0)
-    def _():
-        mlp_half(keep_ref, factors)
+        first_part(keep_ref, factors)
+
+    @pl.when(place_ref[0] != 0)
+    def _():
+        second_part(keep_ref, factors)
 
 
 def mixed_rows(first, second):
@@ -200,19 +200,31 @@
     )
 
 
-def pair_kernel(place_ref, mine_ref, other_ref, dx_ref, out_ref):
-    pack = mine_ref.shape[0]
+def add_rows(out_ref, own, core, dx_ref, other_ref):
     count, tall = dx_ref.shape[:2]
-    own = pack // count
+    short = tall // CORES
+    mine = own + LEAD * short
+    theirs = own + (1 - LEAD) * short
     for to in range(count):
-        rows = slice(to * own, (to + 1) * own)
-        out_ref[to, :own, :] = (mine_ref[rows, :].astype(F32) + other_ref[rows, :].astype(F32)).astype(BF)
-
-    @pl.when(place_ref[0] == 0)
-    def _():
-        for to in range(count):
-            out_ref[to, own : own + tall, :] = dx_ref[to]
-            out_ref[to, own + tall :, :] = other_ref[pack + to * tall : pack + (to + 1) * tall, :]
+        start = count * own + to * tall + core * short
+        out_ref[to, mine : mine + short, :] = dx_ref[to, core * short : (core + 1) * short, :]
+        out_ref[to, theirs : theirs + short, :] = other_ref[start : start + short, :]
+
+
+def pair_kernel(owns, place_ref, mine_ref, other_ref, dx_ref, out_ref):
+    def add(own):
+        for to in range(out_ref.shape[0]):
+            rows = slice(to * own, (to + 1) * own)
+            out_ref[to, :own, :] = (mine_ref[rows, :].astype(F32) + other_ref[rows, :].astype(F32)).astype(BF)
+
+    @pl.when(place_ref[0] == 0)
+    def _():
+        add(owns[0])
+        add_rows(out_ref, owns[0], LEAD, dx_ref, other_ref)
+
+    @pl.when(place_ref[0] != 0)
+    def _():
+        add(owns[1])
 
 
 def total_of(ref, rows):
@@ -222,57 +234,62 @@
     return total.astype(BF)
 
 
-def first_sum_kernel(place_ref, in_ref, out_ref, own_ref, next_ref):
-    own = out_ref.shape[1]
+def spread_total(in_ref, out_ref, own):
     low = total_of(in_ref, own)
-    for i in range(out_ref.shape[0]):
-        out_ref[i] = low
-
-    @pl.when(place_ref[0] == 0)
-    def _():
-        tall = own_ref.shape[0] // (CORES * in_ref.shape[0])
-        for piece in range(in_ref.shape[0]):
-            for core in range(CORES):
-                at = slice((CORES * piece + core) * tall, (CORES * piece + core + 1) * tall)
-                start = own + CORES * core * tall
-                own_ref[at, :] = in_ref[piece, start : start + tall, :]
-                next_ref[at, :] = in_ref[piece, start + tall : start + 2 * tall, :]
-
-
-def second_sum_kernel(in_ref, out_ref):
-    low = total_of(in_ref, in_ref.shape[1])
-    for i in range(out_ref.shape[0]):
-        out_ref[i] = low
-
-
-def join_kernel(mine_ref, next_ref, out_ref):
-    pack = mine_ref.shape[0]
-    out_ref[:pack, :] = mine_ref[...]
-    out_ref[pack:, :] = next_ref[...]
+    for to in range(out_ref.shape[0]):
+        out_ref[to, :own, :] = low
+
+
+def first_sum_kernel(owns, place_ref, in_ref, out_ref):
+    @pl.when(place_ref[0] == 0)
+    def _():
+        spread_total(in_ref, out_ref, owns[0])
+
+    @pl.when(place_ref[0] != 0)
+    def _():
+        spread_total(in_ref, out_ref, owns[1])
+
+
+def second_sum_kernel(owns, place_ref, in_ref, other_ref, dx_ref, out_ref):
+    @pl.when(place_ref[0] == 0)
+    def _():
+        spread_total(in_ref, out_ref, owns[0])
+        add_rows(out_ref, owns[0], 1 - LEAD, dx_ref, other_ref)
+
+    @pl.when(place_ref[0] != 0)
+    def _():
+        spread_total(in_ref, out_ref, owns[1])
 
 
 def finish_kernel(
-    factor, piece, place_ref, mine_ref, other_ref, own_ref, wqkv_ref, wup_ref, gains_ref,
+    factor, owns, place_ref, first_ref, mine_ref, other_ref, wqkv_ref, wup_ref, gains_ref,
     input_ref, qkv_ref, out_ref, up_ref, down_ref, ggains_ref,
 ):
-    pack = mine_ref.shape[0]
     sections, pixels, width = input_ref.shape
 
-    def columns(half, start, ref):
+    def columns(pieces, own, start, ref):
         tall = ref.shape[0]
         for i in range(ref.shape[1] // LANES):
-            ref[:, i * LANES : (i + 1) * LANES] = (
-                half[start + i * tall : start + (i + 1) * tall, :].astype(F32) * factor
-            )
-        return start + tall * (ref.shape[1] // LANES)
-
-    def split(attention, mlp):
-        columns(attention, columns(attention, 0, qkv_ref), out_ref)
-        columns(mlp, columns(mlp, 0, up_ref), down_ref)
-
-    def arrange(rows):
+            row = 0
+            while row < tall:
+                piece, offset = divmod(start + row, own)
+                length = min(own - offset, tall - row)
+                ref[row : row + length, i * LANES : (i + 1) * LANES] = (
+                    pieces[piece, offset : offset + length, :].astype(F32) * factor
+                )
+                row += length
+            start += tall
+        return start
+
+    def split(first, second):
+        columns(first, owns[0], 0, qkv_ref)
+        start = columns(second, owns[1], 0, up_ref)
+        columns(second, owns[1], columns(second, owns[1], start, down_ref), out_ref)
+
+    def arrange(pieces):
         groups = width // LANES
-        blocks = rows.astype(F32).reshape(-1, CORES, piece, LANES)
+        count, tall = pieces.shape[0], sections * pixels * groups // pieces.shape[0]
+        blocks = pieces[:, owns[0] : owns[0] + tall, :].astype(F32).reshape(count, CORES, tall // CORES, LANES)
         tall = blocks.shape[2] // groups
         for i in range(groups):
             at = slice(i * tall, (i + 1) * tall)
@@ -282,12 +299,12 @@
     @pl.when(place_ref[0] == 0)
     def _():
         split(mine_ref, other_ref)
-        arrange(own_ref[...])
+        arrange(first_ref)
 
     @pl.when(place_ref[0] != 0)
     def _():
         split(other_ref, mine_ref)
-        arrange(other_ref[pack:, :])
+        arrange(other_ref)
 
     one = jnp.sum(wqkv_ref[...].astype(F32) * qkv_ref[...], -1)
     two = jnp.sum(wup_ref[...].astype(F32) * up_ref[...], -1)
@@ -315,15 +332,14 @@
     return jax.ShapeDtypeStruct(tuple(dims), kind)
 
 
-def groups_of(axes_by_core):
+def groups_of(lead_axes, other_axes):
     sizes = [lax.axis_size(axis) for axis in AXES]
     groups = {}
-    for core, axes in enumerate(axes_by_core):
-        for index in itertools.product(*map(range, sizes)):
-            at = dict(zip(AXES, index))
-            if at["c"] == core:
-                rest = tuple(at[axis] for axis in AXES if axis not in axes)
-                groups.setdefault((core, rest), []).append((tuple(at[axis] for axis in axes), index))
+    for index in itertools.product(*map(range, sizes)):
+        at = dict(zip(AXES, index))
+        axes = lead_axes if at["c"] == LEAD else other_axes
+        rest = tuple(at[axis] for axis in AXES if axis not in axes)
+        groups.setdefault(rest, []).append((tuple(at[axis] for axis in axes), index))
     flat = lambda index: functools.reduce(lambda total, pair: total * pair[0] + pair[1], zip(sizes, index), 0)
     return [[flat(index) for _, index in sorted(group)] for group in groups.values()]
 
@@ -340,10 +356,9 @@
     peers = lax.axis_size(around)
     near = SIDES * pixels // peers
     hidden = up_weight.shape[1]
-    place = jnp.stack([lax.axis_index("c"), lax.axis_index("l")]).astype(jnp.int32)
+    place = jnp.stack([lax.axis_index("c") ^ LEAD]).astype(jnp.int32)
     zlen = sections * peers // SIDES
     rows = near * zlen
-    pack = (width * 4 * width) // LANES
     chips = peers // CORES
     tall = rows * width // LANES // chips
     both = call(
@@ -367,32 +382,38 @@
         ],
         room=16,
     )
+    wide_groups = groups_of(("x", "h", "l"), ("x", "y"))
+    line_groups = groups_of(("y",), ("l", "h"))
+    slab, line = len(wide_groups[0]), len(line_groups[0])
+    packs = 3 * width * width // LANES, (2 * hidden + width) * width // LANES
+    owns = packs[0] // slab, packs[1] // slab
+    swapped = shape((max(packs[0] + chips * tall, packs[1]), LANES))
+    own = max(owns[0] + tall, owns[1])
     send = call(
-        send_kernel, shape((pack + chips * tall, LANES)), (place, dx, *factors), placed=True, room=12
+        functools.partial(send_kernel, packs[0]), swapped, (place, dx, *factors), placed=True, room=12
     )
     swap = [(0, 1), (1, 0)]
     other = lax.ppermute(send, "c", swap)
-    keep = call(keep_kernel, shape((pack, LANES)), (place, *factors), placed=True, room=12)
-    wide_groups = groups_of((("x", "h", "l"), ("x", "y")))
-    line_groups = groups_of((("y",), ("l", "h")))
-    slab, line = len(wide_groups[0]), len(line_groups[0])
-    own = pack // slab
-    pieces = call(pair_kernel, shape((slab, own + CORES * tall, LANES)), (place, keep, other, dx), placed=True)
-    pieces = exchange(pieces, wide_groups)
-    copies, own_rows, next_rows = call(
-        first_sum_kernel,
-        [shape((line, own, LANES))] + [shape((chips * tall, LANES))] * 2,
-        (place, pieces),
+    keep = call(keep_kernel, shape((max(packs), LANES)), (place, *factors), placed=True, room=12)
+    pieces = call(
+        functools.partial(pair_kernel, owns), shape((slab, own, LANES)), (place, keep, other, dx), placed=True
+    )
+    first = exchange(pieces, wide_groups)
+    copies = call(
+        functools.partial(first_sum_kernel, owns), shape((line, max(owns), LANES)), (place, first), placed=True
+    )
+    pieces = exchange(copies, line_groups)
+    copies = call(
+        functools.partial(second_sum_kernel, owns),
+        shape((slab, own, LANES)),
+        (place, pieces, other, dx),
         placed=True,
     )
-    pieces = exchange(copies, line_groups)
-    copies = call(second_sum_kernel, shape((slab, own, LANES)), (pieces,))
-    mine = exchange(copies, wide_groups).reshape(pack, LANES)
-    joined = call(join_kernel, shape((pack + chips * tall, LANES)), (mine, next_rows))
-    other = lax.ppermute(joined, "c", swap)
+    mine = exchange(copies, wide_groups)
+    other = lax.ppermute(mine, "c", swap)
     voxels = zlen * pixels * lax.axis_size(("y", "l"))
     return tuple(call(
-        functools.partial(finish_kernel, float(voxels) ** (-0.5), tall // CORES),
+        functools.partial(finish_kernel, float(voxels) ** (-0.5), owns),
         [
             shape(features.shape),
             shape((width, 3 * width), F32),
@@ -401,7 +422,7 @@
             shape((hidden, width), F32),
             shape((2, width), F32),
         ],
-        (place, mine, other, own_rows, qkv_weight, up_weight, norm_gains),
+        (place, first, mine, other, qkv_weight, up_weight, norm_gains),
         placed=True,
     ))
 

time: 112 us -> 106 us (0.946)
  Pallas kernels: 13.4 us -> 10.6 us
  starting transfers between devices: 24.3 us -> 22.2 us
  blocking collectives: 53.1 us -> 51.6 us
    pallas_call x9 -> x8, Pallas kernels: 13.4 us -> 10.6 us  [call(): pl.pallas_call(kernel, out_shape=outs, in_specs=specs, out_specs=pl.Block...]
    ppermute x1, starting transfers between devices: 7.11 us -> 5.11 us  [body(): other = lax.ppermute(mine, 'c', swap)]
    all_to_all x3, blocking collectives: 53.1 us -> 51.6 us  [exchange(): lax.all_to_all(pieces, AXES, split_axis=0, concat_axis=0, axis_index_grou...]
  transfers between devices with their start and end apart: 3 -> 3, of which waited for: 3 -> 3; matrix products, arithmetic and copies ran while one was open for 0% -> 0% of each run, Pallas kernels for 1% -> 0%
where the time goes in v5:
time: 106 us
  blocking collectives  51.6 us (49%)
  starting transfers between devices  22.2 us (21%)
  waiting for transfers between devices  20.5 us (19%)
  Pallas kernels  10.6 us (10%)
    all_to_all x3, blocking collectives, exchange(): lax.all_to_all(pieces, AXES, split_axis=0, concat_axis=0, axis_index_grou...  51.6 us
    all_to_all x1, waiting for transfers between devices, body(): xg = lax.all_to_all(both, around, split_axis=0, concat_axis=0, tiled=True)  17.3 us
    all_to_all x1, starting transfers between devices, body(): xg = lax.all_to_all(both, around, split_axis=0, concat_axis=0, tiled=True)  15 us
    pallas_call x8, Pallas kernels, call(): pl.pallas_call(kernel, out_shape=outs, in_specs=specs, out_specs=pl.Block...  10.6 us
    ppermute x1, starting transfers between devices, body(): other = lax.ppermute(mine, 'c', swap)  5.11 us
  transfers between devices with their start and end apart: 3, of which 3 were waited for; matrix products, arithmetic and copies ran while one was open for 0% of the time, Pallas kernels for 0%

profile of v5, /device:TPU:1, one launch (start us, length us, event | category | flops | bytes accessed | tf_op | source)
XLA Modules:
  0.0 105.7 jit_solution(3190866834946987805)
XLA Ops:
  0.6 2.0 %shard_map.118 = bf16[64,16,256]{2,1,0:T(8,128)(2,1)} custom-call(bf16[2,256,256]{2,1,0:T(8,128)(2,1)} %x_hbm.1, bf16[2,256,256]{2,1,0:T(8,128)(2,1)} %g_hbm.1), custom_call_target="tpu_custom_call" | custom-call | tf_op jit(solution)/shard_map/pallas_call | solution.py:319
  2.7 0.0 copy-start
  2.7 0.0 copy-start.1
  2.7 0.0 copy-start.2
  2.7 0.0 copy-start.3
  2.7 15.0 %all-to-all-start = ((bf16[64,16,256]{2,1,0:T(8,128)(2,1)}), bf16[64,16,256]{2,1,0:T(8,128)(2,1)S(1)}, u32[]{:S(2)}, u32[]{:S(2)}) async-start(bf16[64,16,256]{2,1,0:T(8,128)(2,1)} %shard_map.118), calls=%async_computation | async-start | bytes 1048576 | tf_op jit(solution)/shard_map/all_to_all | solution.py:372
  17.7 0.0 copy-start.4
  17.7 17.3 %all-to-all-done.xg_ref = bf16[64,16,256]{2,1,0:T(8,128)(2,1)S(1)} async-done(((bf16[64,16,256]{2,1,0:T(8,128)(2,1)}), bf16[64,16,256]{2,1,0:T(8,128)(2,1)S(1)}, u32[]{:S(2)}, u32[]{:S(2)}) %all-to-all-start) | async-done | bytes 524320 | tf_op jit(solution)/shard_map/all_to_all | solution.py:372
  35.0 0.0 copy-done
  35.0 0.0 copy-done.1
  35.1 5.7 %shard_map.119 = (bf16[32,32,128]{2,1,0:T(8,128)(2,1)S(1)}, bf16[512,256]{1,0:T(8,128)(2,1)S(1)}, bf16[512,768]{1,0:T(8,128)(2,1)S(1)}, bf16[512,256]{1,0:T(8,12...) custom-call(bf16[64,16,256]{2,1,0:T(8,128)(2,1)S(1)} %all-to-all-don, ...), custom_call_target="tpu_custom_call" | custom-call | tf_op jit(solution)/shard_map/pallas_call | solution.py:319
  40.8 0.6 shard_map.121
  41.4 2.1 %collective-permute-start = (bf16[2560,128]{1,0:T(8,128)(2,1)S(1)}, bf16[2560,128]{1,0:T(8,128)(2,1)S(1)}, u32[]{:S(2)}, u32[]{:S(2)}) collective-permute-start(bf16[2560,128]{1,0:T(8,128)(2,1)S(1)} %shard_map.121), channel_id=1, source_target_pairs={{0,1},{1,0},{2,3},{3,2},{4,5},{5,4},{6,7},{7,6},{8,9},{9,8},{10,11... | collective-permute-start | bytes 1966088 | tf_op jit(solution)/shard_map/ppermute | solution.py:396
  43.5 0.4 shard_map.120.mine_ref
  43.9 1.5 %collective-permute-done.other_ref = bf16[2560,128]{1,0:T(8,128)(2,1)S(1)} collective-permute-done((bf16[2560,128]{1,0:T(8,128)(2,1)S(1)}, bf16[2560,128]{1,0:T(8,128)(2,1)S(1)}, u32[]{:S(2)}, u32[]{:S(2)}) %collective-permute-start) | collective-permute-done | bytes 655392 | tf_op jit(solution)/shard_map/ppermute | solution.py:396
  45.4 0.1 shard_map.122
  45.5 18.7 %all_to_all.20.in_ref.first_ref = bf16[32,80,128]{2,1,0:T(8,128)(2,1)S(1)} all-to-all(bf16[32,80,128]{2,1,0:T(8,128)(2,1)S(1)} %shard_map.122), channel_id=1, replica_groups={{0,64,128,192,256,320,384,448,8,72,136,200,264,328,392,456,16,80,144,20..., dimensions={0} | all-to-all | bytes 1310720 | tf_op jit(solution)/shard_map/all_to_all | solution.py:348
  64.2 0.1 shard_map.123
  64.3 14.6 %all_to_all.21.in_ref = bf16[8,80,128]{2,1,0:T(8,128)(2,1)S(1)} all-to-all(bf16[8,80,128]{2,1,0:T(8,128)(2,1)S(1)} %shard_map.123), channel_id=1, replica_groups={{0,2,4,6,32,34,36,38},{1,65,129,193,257,321,385,449},{3,67,131,195,259,..., dimensions={0} | all-to-all | bytes 327680 | tf_op jit(solution)/shard_map/all_to_all | solution.py:348
  78.9 0.1 shard_map.124
  78.9 18.3 %all_to_all.22.mine_ref = bf16[32,80,128]{2,1,0:T(8,128)(2,1)S(1)} all-to-all(bf16[32,80,128]{2,1,0:T(8,128)(2,1)S(1)} %shard_map.124), channel_id=1, replica_groups={{0,64,128,192,256,320,384,448,8,72,136,200,264,328,392,456,16,80,144,20..., dimensions={0} | all-to-all | bytes 1310720 | tf_op jit(solution)/shard_map/all_to_all | solution.py:348
  97.2 5.1 %collective-permute-start.1 = (bf16[32,80,128]{2,1,0:T(8,128)(2,1)S(1)}, bf16[32,80,128]{2,1,0:T(8,128)(2,1)S(1)}, u32[]{:S(2)}, u32[]{:S(2)}) collective-permute-start(bf16[32,80,128]{2,1,0:T(8,128)(2,1)S(1)} %all_to_all.22.mine_ref), channel_id=1, source_target_pairs={{0,1},{1,0},{2,3},{3,2},{4,5},{5,4},{6,7},{7,6},{8,9},{9,8},{10,11... | collective-permute-start | bytes 1966088 | tf_op jit(solution)/shard_map/ppermute | solution.py:413
  102.3 1.7 %collective-permute-done.1.other_ref = bf16[32,80,128]{2,1,0:T(8,128)(2,1)S(1)} collective-permute-done((bf16[32,80,128]{2,1,0:T(8,128)(2,1)S(1)}, bf16[32,80,128]{2,1,0:T(8,128)(2,1)S(1)}, u32[]{:S(2)}, u32[]{:S(2)}) %collective-permute-start.1) | collective-permute-done | bytes 655392 | tf_op jit(solution)/shard_map/ppermute | solution.py:413
  104.0 1.7 %shard_map.125 = (bf16[2,256,256]{2,1,0:T(8,128)(2,1)}, f32[256,768]{1,0:T(8,128)}, f32[256,256]{1,0:T(8,128)}, f32[256,512]{1,0:T(8,128)}, f32[512,256]{1,0:T(8,128)}, /*index=5*/f32[2,256]{1,0:T(2,128)}) custom-call(s32[1]{0:T(128)} %bitcast.place_ref, bf16[32,80,128]{2,1,0:T(8,128)(2,1)S(1)} %all_to_all.20.in_ref.first_ref, ...), custom_call_target="tpu_custom_call" | custom-call | tf_op jit(solution)/shard_map/pallas_call | solution.py:319
  (3 shorter events, 0.0 us)
Async XLA Ops:
  2.7 32.4 %copy-start = (bf16[256,768]{1,0:T(8,128)(2,1)S(1)}, bf16[256,768]{1,0:T(8,128)(2,1)}, u32[]{:S(2)}) copy-start(bf16[256,768]{1,0:T(8,128)(2,1)} %wqkv_ref.3) | copy-start | bytes 1179652
  2.7 32.4 %copy-start.1 = (bf16[256,512]{1,0:T(8,128)(2,1)S(1)}, bf16[256,512]{1,0:T(8,128)(2,1)}, u32[]{:S(2)}) copy-start(bf16[256,512]{1,0:T(8,128)(2,1)} %wup_ref.3) | copy-start | bytes 786436
  2.7 32.3 %copy-start.2 = (bf16[512,256]{1,0:T(8,128)(2,1)S(1)}, bf16[512,256]{1,0:T(8,128)(2,1)}, u32[]{:S(2)}) copy-start(bf16[512,256]{1,0:T(8,128)(2,1)} %wdown_ref.1) | copy-start | bytes 786436
  2.7 32.3 %copy-start.3 = (bf16[256,256]{1,0:T(8,128)(2,1)S(1)}, bf16[256,256]{1,0:T(8,128)(2,1)}, u32[]{:S(2)}) copy-start(bf16[256,256]{1,0:T(8,128)(2,1)} %wout_ref.1) | copy-start | bytes 393220
  2.7 32.3 %all-to-all-start = ((bf16[64,16,256]{2,1,0:T(8,128)(2,1)}), bf16[64,16,256]{2,1,0:T(8,128)(2,1)S(1)}, u32[]{:S(2)}, u32[]{:S(2)}) async-start(bf16[64,16,256]{2,1,0:T(8,128)(2,1)} %shard_map.118), calls=%async_computation | async-start | bytes 1048576 | tf_op jit(solution)/shard_map/all_to_all | solution.py:372
  17.7 17.3 %copy-start.4 = (f32[2,256]{1,0:T(2,128)S(1)}, f32[2,256]{1,0:T(2,128)}, u32[]{:S(2)}) copy-start(f32[2,256]{1,0:T(2,128)} %gains_ref.3) | copy-start | bytes 6148
  41.4 4.0 %collective-permute-start = (bf16[2560,128]{1,0:T(8,128)(2,1)S(1)}, bf16[2560,128]{1,0:T(8,128)(2,1)S(1)}, u32[]{:S(2)}, u32[]{:S(2)}) collective-permute-start(bf16[2560,128]{1,0:T(8,128)(2,1)S(1)} %shard_map.121), channel_id=1, source_target_pairs={{0,1},{1,0},{2,3},{3,2},{4,5},{5,4},{6,7},{7,6},{8,9},{9,8},{10,11... | collective-permute-start | bytes 1966088 | tf_op jit(solution)/shard_map/ppermute | solution.py:396
  97.2 6.8 %collective-permute-start.1 = (bf16[32,80,128]{2,1,0:T(8,128)(2,1)S(1)}, bf16[32,80,128]{2,1,0:T(8,128)(2,1)S(1)}, u32[]{:S(2)}, u32[]{:S(2)}) collective-permute-start(bf16[32,80,128]{2,1,0:T(8,128)(2,1)S(1)} %all_to_all.22.mine_ref), channel_id=1, source_target_pairs={{0,1},{1,0},{2,3},{3,2},{4,5},{5,4},{6,7},{7,6},{8,9},{9,8},{10,11... | collective-permute-start | bytes 1966088 | tf_op jit(solution)/shard_map/ppermute | solution.py:413

commit v6 on v5

--- a/solution.py
+++ b/solution.py
@@ -184,20 +184,35 @@
     return jnp.where(upper, first, turned[1]), jnp.where(upper, turned[0], second)
 
 
-def arrange_kernel(x_hbm, g_hbm, out_ref, x_ref, g_ref, done):
-    peers, _, width = out_ref.shape
-    copies = []
-    for i, (source, target) in enumerate(((x_hbm, x_ref), (g_hbm, g_ref))):
-        for z in range(source.shape[0]):
-            copies.append(pltpu.make_async_copy(source.at[z], target.at[z], done.at[2 * i + z]))
-    for copy in copies:
-        copy.start()
-    for copy in copies:
+def arrange_kernel(x_hbm, g_hbm, out_hbm, x_ref, g_ref, out_ref, come, gone):
+    peers, _, width = out_hbm.shape
+    sections, pixels = x_hbm.shape[:2]
+    parts = gone.shape[0]
+    near, some = pixels // parts, peers // parts
+    coming, going = [], []
+    for part in range(parts):
+        here = slice(part * near, (part + 1) * near)
+        coming.append([
+            pltpu.make_async_copy(source.at[z, here], target.at[z, here], come.at[part, i * sections + z])
+            for i, (source, target) in enumerate(((x_hbm, x_ref), (g_hbm, g_ref)))
+            for z in range(sections)
+        ])
+        for copy in coming[-1]:
+            copy.start()
+    for part in range(parts):
+        here, there = slice(part * near, (part + 1) * near), slice(part * some, (part + 1) * some)
+        for copy in coming[part]:
+            copy.wait()
+        blocks = [
+            mixed_rows(*(ref[z, here].astype(F32).reshape(some // 2, -1, width) for z in range(2)))
+            for ref in (x_ref, g_ref)
+        ]
+        rows = jnp.stack([jnp.concatenate(pair, axis=1) for pair in zip(*blocks)], axis=1)
+        out_ref[there] = rows.reshape(some, -1, width).astype(BF)
+        going.append(pltpu.make_async_copy(out_ref.at[there], out_hbm.at[there], gone.at[part]))
+        going[-1].start()
+    for copy in going:
         copy.wait()
-    parts = [mixed_rows(*(ref[z].astype(F32).reshape(peers // 2, -1, width) for z in range(2))) for ref in (x_ref, g_ref)]
-    out_ref[...] = (
-        jnp.stack([jnp.concatenate(pair, axis=1) for pair in zip(*parts)], axis=1).reshape(out_ref.shape).astype(BF)
-    )
 
 
 def add_rows(out_ref, own, core, dx_ref, other_ref):
@@ -311,7 +326,7 @@
     ggains_ref[...] = jnp.stack([one, two]) / gains_ref[...]
 
 
-def call(kernel, outs, args, scratch=(), placed=False, room=6, spaces=None):
+def call(kernel, outs, args, scratch=(), placed=False, room=6, spaces=None, out_space=pltpu.VMEM):
     specs = [pl.BlockSpec(memory_space=space) for space in spaces or [pltpu.VMEM] * len(args)]
     if placed:
         specs[0] = pl.BlockSpec(memory_space=pltpu.SMEM)
@@ -320,7 +335,7 @@
         kernel,
         out_shape=outs,
         in_specs=specs,
-        out_specs=pl.BlockSpec(memory_space=pltpu.VMEM)
+        out_specs=pl.BlockSpec(memory_space=out_space)
         if single
         else [pl.BlockSpec(memory_space=pltpu.VMEM)] * len(outs),
         scratch_shapes=list(scratch),
@@ -361,12 +376,16 @@
     rows = near * zlen
     chips = peers // CORES
     tall = rows * width // LANES // chips
+    parts = 4
+    given = shape((peers, sections * near, width))
     both = call(
         arrange_kernel,
-        shape((peers, sections * near, width)),
+        given,
         (features, grad_output),
-        scratch=[pltpu.VMEM(features.shape, BF)] * 2 + [pltpu.SemaphoreType.DMA((2 * sections,))],
+        scratch=[pltpu.VMEM(features.shape, BF)] * 2
+        + [pltpu.VMEM(given.shape, BF), pltpu.SemaphoreType.DMA((parts, 2 * sections)), pltpu.SemaphoreType.DMA((parts,))],
         spaces=[pl.ANY, pl.ANY],
+        out_space=pltpu.HBM,
         room=60,
     )
     xg = lax.all_to_all(both, around, split_axis=0, concat_axis=0, tiled=True)

time: 106 us -> 106 us (level)
  no operation moved by 1% of the time
where the time goes in v6:
time: 106 us; the launch traced here: 105 us
  blocking collectives  51.6 us (49%)
  starting transfers between devices  22.2 us (21%)
  waiting for transfers between devices  20.5 us (19%)
  Pallas kernels  10.5 us (10%)
    all_to_all x3, blocking collectives, exchange(): lax.all_to_all(pieces, AXES, split_axis=0, concat_axis=0, axis_index_grou...  51.6 us
    all_to_all x1, waiting for transfers between devices, body(): xg = lax.all_to_all(both, around, split_axis=0, concat_axis=0, tiled=True)  17.3 us
    all_to_all x1, starting transfers between devices, body(): xg = lax.all_to_all(both, around, split_axis=0, concat_axis=0, tiled=True)  15 us
    pallas_call x8, Pallas kernels, call(): pl.pallas_call(kernel, out_shape=outs, in_specs=specs, out_specs=pl.Block...  10.5 us
    ppermute x1, starting transfers between devices, body(): other = lax.ppermute(mine, 'c', swap)  5.11 us
  transfers between devices with their start and end apart: 3, of which 3 were waited for; matrix products, arithmetic and copies ran while one was open for 0% of the time, Pallas kernels for 0%

profile of v6, /device:TPU:1, one launch (start us, length us, event | category | flops | bytes accessed | tf_op | source)
XLA Modules:
  0.0 105.5 jit_solution(4995925706729573311)
XLA Ops:
  0.6 1.9 %shard_map.118 = bf16[64,16,256]{2,1,0:T(8,128)(2,1)} custom-call(bf16[2,256,256]{2,1,0:T(8,128)(2,1)} %x_hbm.1, bf16[2,256,256]{2,1,0:T(8,128)(2,1)} %g_hbm.1), custom_call_target="tpu_custom_call" | custom-call | tf_op jit(solution)/shard_map/pallas_call | solution.py:334
  2.5 0.0 copy-start
  2.5 0.0 copy-start.1
  2.5 0.0 copy-start.2
  2.5 0.0 copy-start.3
  2.5 15.0 %all-to-all-start = ((bf16[64,16,256]{2,1,0:T(8,128)(2,1)}), bf16[64,16,256]{2,1,0:T(8,128)(2,1)S(1)}, u32[]{:S(2)}, u32[]{:S(2)}) async-start(bf16[64,16,256]{2,1,0:T(8,128)(2,1)} %shard_map.118), calls=%async_computation | async-start | bytes 1048576 | tf_op jit(solution)/shard_map/all_to_all | solution.py:391
  17.5 0.0 copy-start.4
  17.6 17.3 %all-to-all-done.xg_ref = bf16[64,16,256]{2,1,0:T(8,128)(2,1)S(1)} async-done(((bf16[64,16,256]{2,1,0:T(8,128)(2,1)}), bf16[64,16,256]{2,1,0:T(8,128)(2,1)S(1)}, u32[]{:S(2)}, u32[]{:S(2)}) %all-to-all-start) | async-done | bytes 524320 | tf_op jit(solution)/shard_map/all_to_all | solution.py:391
  34.9 0.0 copy-done
  34.9 0.0 copy-done.2
  34.9 5.7 %shard_map.119 = (bf16[32,32,128]{2,1,0:T(8,128)(2,1)S(1)}, bf16[512,256]{1,0:T(8,128)(2,1)S(1)}, bf16[512,768]{1,0:T(8,128)(2,1)S(1)}, bf16[512,256]{1,0:T(8,12...) custom-call(bf16[64,16,256]{2,1,0:T(8,128)(2,1)S(1)} %all-to-all-don, ...), custom_call_target="tpu_custom_call" | custom-call | tf_op jit(solution)/shard_map/pallas_call | solution.py:334
  40.6 0.6 shard_map.121
  41.2 2.1 %collective-permute-start = (bf16[2560,128]{1,0:T(8,128)(2,1)S(1)}, bf16[2560,128]{1,0:T(8,128)(2,1)S(1)}, u32[]{:S(2)}, u32[]{:S(2)}) collective-permute-start(bf16[2560,128]{1,0:T(8,128)(2,1)S(1)} %shard_map.121), channel_id=1, source_target_pairs={{0,1},{1,0},{2,3},{3,2},{4,5},{5,4},{6,7},{7,6},{8,9},{9,8},{10,11... | collective-permute-start | bytes 1966088 | tf_op jit(solution)/shard_map/ppermute | solution.py:415
  43.3 0.4 shard_map.120.mine_ref
  43.7 1.5 %collective-permute-done.other_ref = bf16[2560,128]{1,0:T(8,128)(2,1)S(1)} collective-permute-done((bf16[2560,128]{1,0:T(8,128)(2,1)S(1)}, bf16[2560,128]{1,0:T(8,128)(2,1)S(1)}, u32[]{:S(2)}, u32[]{:S(2)}) %collective-permute-start) | collective-permute-done | bytes 655392 | tf_op jit(solution)/shard_map/ppermute | solution.py:415
  45.2 0.1 shard_map.122
  45.3 18.7 %all_to_all.20.in_ref.first_ref = bf16[32,80,128]{2,1,0:T(8,128)(2,1)S(1)} all-to-all(bf16[32,80,128]{2,1,0:T(8,128)(2,1)S(1)} %shard_map.122), channel_id=1, replica_groups={{0,64,128,192,256,320,384,448,8,72,136,200,264,328,392,456,16,80,144,20..., dimensions={0} | all-to-all | bytes 1310720 | tf_op jit(solution)/shard_map/all_to_all | solution.py:363
  64.0 0.1 shard_map.123
  64.1 14.6 %all_to_all.21.in_ref = bf16[8,80,128]{2,1,0:T(8,128)(2,1)S(1)} all-to-all(bf16[8,80,128]{2,1,0:T(8,128)(2,1)S(1)} %shard_map.123), channel_id=1, replica_groups={{0,2,4,6,32,34,36,38},{1,65,129,193,257,321,385,449},{3,67,131,195,259,..., dimensions={0} | all-to-all | bytes 327680 | tf_op jit(solution)/shard_map/all_to_all | solution.py:363
  78.7 0.1 shard_map.124
  78.7 18.3 %all_to_all.22.mine_ref = bf16[32,80,128]{2,1,0:T(8,128)(2,1)S(1)} all-to-all(bf16[32,80,128]{2,1,0:T(8,128)(2,1)S(1)} %shard_map.124), channel_id=1, replica_groups={{0,64,128,192,256,320,384,448,8,72,136,200,264,328,392,456,16,80,144,20..., dimensions={0} | all-to-all | bytes 1310720 | tf_op jit(solution)/shard_map/all_to_all | solution.py:363
  97.0 5.1 %collective-permute-start.1 = (bf16[32,80,128]{2,1,0:T(8,128)(2,1)S(1)}, bf16[32,80,128]{2,1,0:T(8,128)(2,1)S(1)}, u32[]{:S(2)}, u32[]{:S(2)}) collective-permute-start(bf16[32,80,128]{2,1,0:T(8,128)(2,1)S(1)} %all_to_all.22.mine_ref), channel_id=1, source_target_pairs={{0,1},{1,0},{2,3},{3,2},{4,5},{5,4},{6,7},{7,6},{8,9},{9,8},{10,11... | collective-permute-start | bytes 1966088 | tf_op jit(solution)/shard_map/ppermute | solution.py:432
  102.1 1.7 %collective-permute-done.1.other_ref = bf16[32,80,128]{2,1,0:T(8,128)(2,1)S(1)} collective-permute-done((bf16[32,80,128]{2,1,0:T(8,128)(2,1)S(1)}, bf16[32,80,128]{2,1,0:T(8,128)(2,1)S(1)}, u32[]{:S(2)}, u32[]{:S(2)}) %collective-permute-start.1) | collective-permute-done | bytes 655392 | tf_op jit(solution)/shard_map/ppermute | solution.py:432
  103.8 1.7 %shard_map.125 = (bf16[2,256,256]{2,1,0:T(8,128)(2,1)}, f32[256,768]{1,0:T(8,128)}, f32[256,256]{1,0:T(8,128)}, f32[256,512]{1,0:T(8,128)}, f32[512,256]{1,0:T(8,128)}, /*index=5*/f32[2,256]{1,0:T(2,128)}) custom-call(s32[1]{0:T(128)} %bitcast.place_ref, bf16[32,80,128]{2,1,0:T(8,128)(2,1)S(1)} %all_to_all.20.in_ref.first_ref, ...), custom_call_target="tpu_custom_call" | custom-call | tf_op jit(solution)/shard_map/pallas_call | solution.py:334
  (3 shorter events, 0.0 us)
Async XLA Ops:
  2.5 32.4 %copy-start = (bf16[256,768]{1,0:T(8,128)(2,1)S(1)}, bf16[256,768]{1,0:T(8,128)(2,1)}, u32[]{:S(2)}) copy-start(bf16[256,768]{1,0:T(8,128)(2,1)} %wqkv_ref.3) | copy-start | bytes 1179652
  2.5 32.4 %copy-start.1 = (bf16[256,512]{1,0:T(8,128)(2,1)S(1)}, bf16[256,512]{1,0:T(8,128)(2,1)}, u32[]{:S(2)}) copy-start(bf16[256,512]{1,0:T(8,128)(2,1)} %wup_ref.3) | copy-start | bytes 786436
  2.5 32.3 %copy-start.2 = (bf16[512,256]{1,0:T(8,128)(2,1)S(1)}, bf16[512,256]{1,0:T(8,128)(2,1)}, u32[]{:S(2)}) copy-start(bf16[512,256]{1,0:T(8,128)(2,1)} %wdown_ref.1) | copy-start | bytes 786436
  2.5 32.3 %copy-start.3 = (bf16[256,256]{1,0:T(8,128)(2,1)S(1)}, bf16[256,256]{1,0:T(8,128)(2,1)}, u32[]{:S(2)}) copy-start(bf16[256,256]{1,0:T(8,128)(2,1)} %wout_ref.1) | copy-start | bytes 393220
  2.5 32.3 %all-to-all-start = ((bf16[64,16,256]{2,1,0:T(8,128)(2,1)}), bf16[64,16,256]{2,1,0:T(8,128)(2,1)S(1)}, u32[]{:S(2)}, u32[]{:S(2)}) async-start(bf16[64,16,256]{2,1,0:T(8,128)(2,1)} %shard_map.118), calls=%async_computation | async-start | bytes 1048576 | tf_op jit(solution)/shard_map/all_to_all | solution.py:391
  17.5 17.3 %copy-start.4 = (f32[2,256]{1,0:T(2,128)S(1)}, f32[2,256]{1,0:T(2,128)}, u32[]{:S(2)}) copy-start(f32[2,256]{1,0:T(2,128)} %gains_ref.3) | copy-start | bytes 6148
  41.2 4.0 %collective-permute-start = (bf16[2560,128]{1,0:T(8,128)(2,1)S(1)}, bf16[2560,128]{1,0:T(8,128)(2,1)S(1)}, u32[]{:S(2)}, u32[]{:S(2)}) collective-permute-start(bf16[2560,128]{1,0:T(8,128)(2,1)S(1)} %shard_map.121), channel_id=1, source_target_pairs={{0,1},{1,0},{2,3},{3,2},{4,5},{5,4},{6,7},{7,6},{8,9},{9,8},{10,11... | collective-permute-start | bytes 1966088 | tf_op jit(solution)/shard_map/ppermute | solution.py:415
  97.0 6.8 %collective-permute-start.1 = (bf16[32,80,128]{2,1,0:T(8,128)(2,1)S(1)}, bf16[32,80,128]{2,1,0:T(8,128)(2,1)S(1)}, u32[]{:S(2)}, u32[]{:S(2)}) collective-permute-start(bf16[32,80,128]{2,1,0:T(8,128)(2,1)S(1)} %all_to_all.22.mine_ref), channel_id=1, source_target_pairs={{0,1},{1,0},{2,3},{3,2},{4,5},{5,4},{6,7},{7,6},{8,9},{9,8},{10,11... | collective-permute-start | bytes 1966088 | tf_op jit(solution)/shard_map/ppermute | solution.py:432

commit v7 on v6

--- a/solution.py
+++ b/solution.py
@@ -277,49 +277,54 @@
 
 
 def finish_kernel(
-    factor, owns, place_ref, first_ref, mine_ref, other_ref, wqkv_ref, wup_ref, gains_ref,
+    factor, owns, parts, place_ref, first_ref, mine_ref, other_ref, wqkv_ref, wup_ref, gains_ref,
     input_ref, qkv_ref, out_ref, up_ref, down_ref, ggains_ref,
 ):
     sections, pixels, width = input_ref.shape
 
-    def columns(pieces, own, start, ref):
+    def columns(part, pieces, own, start, ref):
         tall = ref.shape[0]
         for i in range(ref.shape[1] // LANES):
             row = 0
             while row < tall:
-                piece, offset = divmod(start + row, own)
+                piece, offset = divmod(start + part * tall + row, own)
                 length = min(own - offset, tall - row)
                 ref[row : row + length, i * LANES : (i + 1) * LANES] = (
                     pieces[piece, offset : offset + length, :].astype(F32) * factor
                 )
                 row += length
-            start += tall
+            start += parts * tall
         return start
 
-    def split(first, second):
-        columns(first, owns[0], 0, qkv_ref)
-        start = columns(second, owns[1], 0, up_ref)
-        columns(second, owns[1], columns(second, owns[1], start, down_ref), out_ref)
-
-    def arrange(pieces):
+    def split(part, first, second):
+        columns(part, first, owns[0], 0, qkv_ref)
+        start = columns(part, second, owns[1], 0, up_ref)
+        start = columns(part, second, owns[1], start, down_ref)
+        columns(part, second, owns[1], start, out_ref)
+
+    def arrange(part, pieces):
         groups = width // LANES
-        count, tall = pieces.shape[0], sections * pixels * groups // pieces.shape[0]
-        blocks = pieces[:, owns[0] : owns[0] + tall, :].astype(F32).reshape(count, CORES, tall // CORES, LANES)
+        count = pieces.shape[0] // parts
+        tall = sections * pixels * groups // count
+        here = pieces[part * count : (part + 1) * count, owns[0] : owns[0] + tall, :]
+        blocks = here.astype(F32).reshape(count, CORES, tall // CORES, LANES)
         tall = blocks.shape[2] // groups
         for i in range(groups):
             at = slice(i * tall, (i + 1) * tall)
             for z, block in enumerate(mixed_rows(blocks[:, 0, at, :], blocks[:, 1, at, :])):
                 input_ref[z, :, i * LANES : (i + 1) * LANES] = block.reshape(pixels, LANES).astype(BF)
 
-    @pl.when(place_ref[0] == 0)
-    def _():
-        split(mine_ref, other_ref)
-        arrange(first_ref)
-
-    @pl.when(place_ref[0] != 0)
-    def _():
-        split(other_ref, mine_ref)
-        arrange(other_ref)
+    for part in range(parts):
+
+        @pl.when((pl.program_id(0) == part) & (place_ref[0] == 0))
+        def _():
+            split(part, mine_ref, other_ref)
+            arrange(part, first_ref)
+
+        @pl.when((pl.program_id(0) == part) & (place_ref[0] != 0))
+        def _():
+            split(part, other_ref, mine_ref)
+            arrange(part, other_ref)
 
     one = jnp.sum(wqkv_ref[...].astype(F32) * qkv_ref[...], -1)
     two = jnp.sum(wup_ref[...].astype(F32) * up_ref[...], -1)
@@ -431,9 +436,14 @@
     mine = exchange(copies, wide_groups)
     other = lax.ppermute(mine, "c", swap)
     voxels = zlen * pixels * lax.axis_size(("y", "l"))
-    return tuple(call(
-        functools.partial(finish_kernel, float(voxels) ** (-0.5), owns),
-        [
+    parts = 2
+    whole = pl.BlockSpec(memory_space=pltpu.VMEM)
+    rows = lambda tall, wide: pl.BlockSpec((tall // parts, wide), lambda i: (i, 0))
+    gains = pl.BlockSpec((2, width // parts), lambda i: (0, i))
+    return tuple(pl.pallas_call(
+        functools.partial(finish_kernel, float(voxels) ** (-0.5), owns, parts),
+        grid=(parts,),
+        out_shape=[
             shape(features.shape),
             shape((width, 3 * width), F32),
             shape((width, width), F32),
@@ -441,9 +451,25 @@
             shape((hidden, width), F32),
             shape((2, width), F32),
         ],
-        (place, first, mine, other, qkv_weight, up_weight, norm_gains),
-        placed=True,
-    ))
+        in_specs=[
+            pl.BlockSpec(memory_space=pltpu.SMEM),
+            whole,
+            whole,
+            whole,
+            rows(width, 3 * width),
+            rows(width, hidden),
+            gains,
+        ],
+        out_specs=[
+            pl.BlockSpec((sections, pixels // parts, width), lambda i: (0, i, 0)),
+            rows(width, 3 * width),
+            rows(width, width),
+            rows(width, hidden),
+            rows(hidden, width),
+            gains,
+        ],
+        compiler_params=pltpu.CompilerParams(vmem_limit_bytes=12 * MIB),
+    )(place, first, mine, other, qkv_weight, up_weight, norm_gains))
 
 
 def solution(mesh):

time: 106 us -> 106 us (level)
    pallas_call x0 -> x1, Pallas kernels: none -> 1.68 us  [body(): pl.pallas_call(functools.partial(finish_kernel, float(voxels) ** (-0.5),...]
    pallas_call x8 -> x7, Pallas kernels: 10.5 us -> 8.8 us  [call(): pl.pallas_call(kernel, out_shape=outs, in_specs=specs, out_specs=pl.Block...]
where the time goes in v7:
time: 106 us
  blocking collectives  51.6 us (49%)
  starting transfers between devices  22.2 us (21%)
  waiting for transfers between devices  20.5 us (19%)
  Pallas kernels  10.5 us (10%)
    all_to_all x3, blocking collectives, exchange(): lax.all_to_all(pieces, AXES, split_axis=0, concat_axis=0, axis_index_grou...  51.6 us
    all_to_all x1, waiting for transfers between devices, body(): xg = lax.all_to_all(both, around, split_axis=0, concat_axis=0, tiled=True)  17.3 us
    all_to_all x1, starting transfers between devices, body(): xg = lax.all_to_all(both, around, split_axis=0, concat_axis=0, tiled=True)  15 us
    pallas_call x7, Pallas kernels, call(): pl.pallas_call(kernel, out_shape=outs, in_specs=specs, out_specs=pl.Block...  8.8 us
    ppermute x1, starting transfers between devices, body(): other = lax.ppermute(mine, 'c', swap)  5.11 us
  transfers between devices with their start and end apart: 3, of which 3 were waited for; matrix products, arithmetic and copies ran while one was open for 0% of the time, Pallas kernels for 0%

profile of v7, /device:TPU:1, one launch (start us, length us, event | category | flops | bytes accessed | tf_op | source)
XLA Modules:
  0.0 105.5 jit_solution(11388019006681616874)
XLA Ops:
  0.6 1.9 %shard_map.118 = bf16[64,16,256]{2,1,0:T(8,128)(2,1)} custom-call(bf16[2,256,256]{2,1,0:T(8,128)(2,1)} %x_hbm.1, bf16[2,256,256]{2,1,0:T(8,128)(2,1)} %g_hbm.1), custom_call_target="tpu_custom_call" | custom-call | tf_op jit(solution)/shard_map/pallas_call | solution.py:339
  2.5 0.0 copy-start
  2.5 0.0 copy-start.1
  2.5 0.0 copy-start.2
  2.5 0.0 copy-start.3
  2.5 15.0 %all-to-all-start = ((bf16[64,16,256]{2,1,0:T(8,128)(2,1)}), bf16[64,16,256]{2,1,0:T(8,128)(2,1)S(1)}, u32[]{:S(2)}, u32[]{:S(2)}) async-start(bf16[64,16,256]{2,1,0:T(8,128)(2,1)} %shard_map.118), calls=%async_computation | async-start | bytes 1048576 | tf_op jit(solution)/shard_map/all_to_all | solution.py:396
  17.5 0.0 copy-start.4
  17.6 17.3 %all-to-all-done.xg_ref = bf16[64,16,256]{2,1,0:T(8,128)(2,1)S(1)} async-done(((bf16[64,16,256]{2,1,0:T(8,128)(2,1)}), bf16[64,16,256]{2,1,0:T(8,128)(2,1)S(1)}, u32[]{:S(2)}, u32[]{:S(2)}) %all-to-all-start) | async-done | bytes 524320 | tf_op jit(solution)/shard_map/all_to_all | solution.py:396
  34.9 0.0 copy-done
  34.9 0.0 copy-done.1
  34.9 5.7 %shard_map.119 = (bf16[32,32,128]{2,1,0:T(8,128)(2,1)S(1)}, bf16[512,256]{1,0:T(8,128)(2,1)S(1)}, bf16[512,768]{1,0:T(8,128)(2,1)S(1)}, bf16[512,256]{1,0:T(8,12...) custom-call(bf16[64,16,256]{2,1,0:T(8,128)(2,1)S(1)} %all-to-all-don, ...), custom_call_target="tpu_custom_call" | custom-call | tf_op jit(solution)/shard_map/pallas_call | solution.py:339
  40.6 0.6 shard_map.121
  41.2 2.1 %collective-permute-start = (bf16[2560,128]{1,0:T(8,128)(2,1)S(1)}, bf16[2560,128]{1,0:T(8,128)(2,1)S(1)}, u32[]{:S(2)}, u32[]{:S(2)}) collective-permute-start(bf16[2560,128]{1,0:T(8,128)(2,1)S(1)} %shard_map.121), channel_id=1, source_target_pairs={{0,1},{1,0},{2,3},{3,2},{4,5},{5,4},{6,7},{7,6},{8,9},{9,8},{10,11... | collective-permute-start | bytes 1966088 | tf_op jit(solution)/shard_map/ppermute | solution.py:420
  43.3 0.4 shard_map.120.mine_ref
  43.7 1.5 %collective-permute-done.other_ref = bf16[2560,128]{1,0:T(8,128)(2,1)S(1)} collective-permute-done((bf16[2560,128]{1,0:T(8,128)(2,1)S(1)}, bf16[2560,128]{1,0:T(8,128)(2,1)S(1)}, u32[]{:S(2)}, u32[]{:S(2)}) %collective-permute-start) | collective-permute-done | bytes 655392 | tf_op jit(solution)/shard_map/ppermute | solution.py:420
  45.2 0.1 shard_map.122
  45.3 18.7 %all_to_all.20.in_ref.first_ref = bf16[32,80,128]{2,1,0:T(8,128)(2,1)S(1)} all-to-all(bf16[32,80,128]{2,1,0:T(8,128)(2,1)S(1)} %shard_map.122), channel_id=1, replica_groups={{0,64,128,192,256,320,384,448,8,72,136,200,264,328,392,456,16,80,144,20..., dimensions={0} | all-to-all | bytes 1310720 | tf_op jit(solution)/shard_map/all_to_all | solution.py:368
  64.0 0.1 shard_map.123
  64.1 14.6 %all_to_all.21.in_ref = bf16[8,80,128]{2,1,0:T(8,128)(2,1)S(1)} all-to-all(bf16[8,80,128]{2,1,0:T(8,128)(2,1)S(1)} %shard_map.123), channel_id=1, replica_groups={{0,2,4,6,32,34,36,38},{1,65,129,193,257,321,385,449},{3,67,131,195,259,..., dimensions={0} | all-to-all | bytes 327680 | tf_op jit(solution)/shard_map/all_to_all | solution.py:368
  78.7 0.1 shard_map.124
  78.7 18.3 %all_to_all.22.mine_ref = bf16[32,80,128]{2,1,0:T(8,128)(2,1)S(1)} all-to-all(bf16[32,80,128]{2,1,0:T(8,128)(2,1)S(1)} %shard_map.124), channel_id=1, replica_groups={{0,64,128,192,256,320,384,448,8,72,136,200,264,328,392,456,16,80,144,20..., dimensions={0} | all-to-all | bytes 1310720 | tf_op jit(solution)/shard_map/all_to_all | solution.py:368
  97.0 5.1 %collective-permute-start.1 = (bf16[32,80,128]{2,1,0:T(8,128)(2,1)S(1)}, bf16[32,80,128]{2,1,0:T(8,128)(2,1)S(1)}, u32[]{:S(2)}, u32[]{:S(2)}) collective-permute-start(bf16[32,80,128]{2,1,0:T(8,128)(2,1)S(1)} %all_to_all.22.mine_ref), channel_id=1, source_target_pairs={{0,1},{1,0},{2,3},{3,2},{4,5},{5,4},{6,7},{7,6},{8,9},{9,8},{10,11... | collective-permute-start | bytes 1966088 | tf_op jit(solution)/shard_map/ppermute | solution.py:437
  102.1 1.7 %collective-permute-done.1.other_ref = bf16[32,80,128]{2,1,0:T(8,128)(2,1)S(1)} collective-permute-done((bf16[32,80,128]{2,1,0:T(8,128)(2,1)S(1)}, bf16[32,80,128]{2,1,0:T(8,128)(2,1)S(1)}, u32[]{:S(2)}, u32[]{:S(2)}) %collective-permute-start.1) | collective-permute-done | bytes 655392 | tf_op jit(solution)/shard_map/ppermute | solution.py:437
  103.8 1.7 %shard_map.125 = (bf16[2,256,256]{2,1,0:T(8,128)(2,1)}, f32[256,768]{1,0:T(8,128)}, f32[256,256]{1,0:T(8,128)}, f32[256,512]{1,0:T(8,128)}, f32[512,256]{1,0:T(8,128)}, /*index=5*/f32[2,256]{1,0:T(2,128)}) custom-call(s32[1]{0:T(128)} %bitcast.place_ref, bf16[32,80,128]{2,1,0:T(8,128)(2,1)S(1)} %all_to_all.20.in_ref.first_ref, ...), custom_call_target="tpu_custom_call" | custom-call | tf_op jit(solution)/shard_map/pallas_call | solution.py:443
  (3 shorter events, 0.0 us)
Async XLA Ops:
  2.5 32.4 %copy-start = (bf16[256,768]{1,0:T(8,128)(2,1)S(1)}, bf16[256,768]{1,0:T(8,128)(2,1)}, u32[]{:S(2)}) copy-start(bf16[256,768]{1,0:T(8,128)(2,1)} %wqkv_ref.3) | copy-start | bytes 1179652
  2.5 32.4 %copy-start.1 = (bf16[256,512]{1,0:T(8,128)(2,1)S(1)}, bf16[256,512]{1,0:T(8,128)(2,1)}, u32[]{:S(2)}) copy-start(bf16[256,512]{1,0:T(8,128)(2,1)} %wup_ref.3) | copy-start | bytes 786436
  2.5 32.3 %copy-start.2 = (bf16[512,256]{1,0:T(8,128)(2,1)S(1)}, bf16[512,256]{1,0:T(8,128)(2,1)}, u32[]{:S(2)}) copy-start(bf16[512,256]{1,0:T(8,128)(2,1)} %wdown_ref.1) | copy-start | bytes 786436
  2.5 32.3 %copy-start.3 = (bf16[256,256]{1,0:T(8,128)(2,1)S(1)}, bf16[256,256]{1,0:T(8,128)(2,1)}, u32[]{:S(2)}) copy-start(bf16[256,256]{1,0:T(8,128)(2,1)} %wout_ref.1) | copy-start | bytes 393220
  2.5 32.3 %all-to-all-start = ((bf16[64,16,256]{2,1,0:T(8,128)(2,1)}), bf16[64,16,256]{2,1,0:T(8,128)(2,1)S(1)}, u32[]{:S(2)}, u32[]{:S(2)}) async-start(bf16[64,16,256]{2,1,0:T(8,128)(2,1)} %shard_map.118), calls=%async_computation | async-start | bytes 1048576 | tf_op jit(solution)/shard_map/all_to_all | solution.py:396
  17.5 17.3 %copy-start.4 = (f32[2,256]{1,0:T(2,128)S(1)}, f32[2,256]{1,0:T(2,128)}, u32[]{:S(2)}) copy-start(f32[2,256]{1,0:T(2,128)} %gains_ref.3) | copy-start | bytes 6148
  41.2 4.0 %collective-permute-start = (bf16[2560,128]{1,0:T(8,128)(2,1)S(1)}, bf16[2560,128]{1,0:T(8,128)(2,1)S(1)}, u32[]{:S(2)}, u32[]{:S(2)}) collective-permute-start(bf16[2560,128]{1,0:T(8,128)(2,1)S(1)} %shard_map.121), channel_id=1, source_target_pairs={{0,1},{1,0},{2,3},{3,2},{4,5},{5,4},{6,7},{7,6},{8,9},{9,8},{10,11... | collective-permute-start | bytes 1966088 | tf_op jit(solution)/shard_map/ppermute | solution.py:420
  97.0 6.8 %collective-permute-start.1 = (bf16[32,80,128]{2,1,0:T(8,128)(2,1)S(1)}, bf16[32,80,128]{2,1,0:T(8,128)(2,1)S(1)}, u32[]{:S(2)}, u32[]{:S(2)}) collective-permute-start(bf16[32,80,128]{2,1,0:T(8,128)(2,1)S(1)} %all_to_all.22.mine_ref), channel_id=1, source_target_pairs={{0,1},{1,0},{2,3},{3,2},{4,5},{5,4},{6,7},{7,6},{8,9},{9,8},{10,11... | collective-permute-start | bytes 1966088 | tf_op jit(solution)/shard_map/ppermute | solution.py:437
